TPU v7x, 128 devices: a whole 4x4x4 slice. The times are simulated.
128 devices in a mesh: win: 4 (over z_hi, core), chan: 32 (over x, z_lo, y).
Axes of the slice: x: 4, y: 4, z: 4 (z_hi: 2, z_lo: 2; z = z_hi * 2 + z_lo), core: 2. Of those that a mesh axis runs over, the one named last changes fastest.
Arguments:
- record: bfloat16 [12, 7936, 8192], P('win', 'chan'), may hold values from -6 to 6
- offsets: int32 [12], P('win'), may hold values from 0 to 256
- sources: int32 [3, 16], replicated, may hold values from 0 to 8191
Outputs:
- correlations: bfloat16 [3, 16, 256, 8192], P(None, 'win', None, 'chan')
Inputs may be any that keep to these rules, and one draw needn't show every extreme that they name: `sources`: channels may repeat within a round.
All inputs are finite; a program needn't handle non-finite values.
Results may differ from a plain program's by a relative error of at most 0.0061.
Values may be sent and summed in bfloat16 or wider, within the bound.
A program may use at most 192 MiB of HBM per device.

v0:
```python
import math

import jax
import jax.numpy as jnp
from jax import lax
from jax.sharding import PartitionSpec as P

SAMPLES = 7680
BINS = 256
F0 = 16
LAGS = 256
LAG_STEP = 8
ROUNDS = 3


def dft_table():
    steps = jnp.arange(SAMPLES, dtype=jnp.int32)
    freqs = jnp.arange(BINS, dtype=jnp.int32) + F0
    phase = freqs[:, None] * steps[None, :] % SAMPLES
    angle = 2.0 * math.pi / SAMPLES * phase.astype(jnp.float32)
    taper = 0.5 - 0.5 * jnp.cos(2.0 * math.pi / SAMPLES * steps.astype(jnp.float32))
    rows = jnp.concatenate(
        [taper[None, :] * jnp.cos(angle), -taper[None, :] * jnp.sin(angle)], axis=0
    )
    return rows.astype(jnp.bfloat16)


def lag_tables():
    lag_ids = jnp.arange(LAGS, dtype=jnp.int32)
    shifts = LAG_STEP * (lag_ids - LAGS // 2)
    freqs = jnp.arange(BINS, dtype=jnp.int32) + F0
    phase = shifts[:, None] * freqs[None, :] % SAMPLES
    angle = 2.0 * math.pi / SAMPLES * phase.astype(jnp.float32)
    return (jnp.cos(angle), jnp.sin(angle))


def make_kernel(chosen, scale):
    cos_lag, sin_lag = lag_tables()
    real_part = chosen[:, :BINS, :]
    imag_part = chosen[:, BINS:, :]
    high = lax.Precision.HIGHEST
    first = jnp.einsum("wfs,kf->skwf", real_part, cos_lag, precision=high) + jnp.einsum(
        "wfs,kf->skwf", imag_part, sin_lag, precision=high
    )
    second = jnp.einsum("wfs,kf->skwf", imag_part, cos_lag, precision=high) - jnp.einsum(
        "wfs,kf->skwf", real_part, sin_lag, precision=high
    )
    joined = jnp.concatenate([first, second], axis=3) * scale
    count = chosen.shape[2]
    return joined.reshape(count * LAGS, chosen.shape[0] * 2 * BINS).astype(jnp.bfloat16)


def select_columns(base, wanted, first_channel):
    width = base.shape[2]
    column_ids = jnp.arange(width, dtype=jnp.int32)
    onehot = (wanted[:, None, :] - first_channel == column_ids[None, :, None]).astype(jnp.bfloat16)
    return jnp.einsum("wfc,rcs->rwfs", base, onehot, preferred_element_type=jnp.float32)


def body(record, offsets, sources):
    local = lax.all_to_all(record, "chan", split_axis=2, concat_axis=1, tiled=True)
    local_windows = local.shape[0]
    width = local.shape[2]
    first_channel = lax.axis_index("chan") * width
    table = dft_table()
    spectra = []
    for window in range(local_windows):
        segment = lax.dynamic_slice_in_dim(local[window], offsets[window], SAMPLES, 0)
        spectra.append(jnp.dot(table, segment, preferred_element_type=jnp.float32))
    spectra = jnp.stack(spectra, axis=0)
    power = jnp.mean(spectra * spectra, axis=1, keepdims=True)
    white = (spectra * lax.rsqrt(power + 1e-06)).astype(jnp.bfloat16)
    total_windows = local_windows * lax.axis_size("win")
    scale = 1.0 / math.sqrt(total_windows * BINS)
    flat = white.reshape(white.shape[0] * 2 * BINS, width)
    results = []
    for step in range(ROUNDS):
        chosen = lax.psum(
            select_columns(white, sources[step : step + 1], first_channel)[0].astype(jnp.bfloat16),
            "chan",
        ).astype(jnp.float32)
        kernel = make_kernel(chosen, scale)
        joint = jnp.dot(kernel, flat, preferred_element_type=jnp.float32)
        share = lax.psum_scatter(joint, "win", scatter_dimension=0, tiled=True)
        results.append(share.astype(jnp.bfloat16).reshape(-1, LAGS, width))
    return jnp.stack(results, axis=0)


def solution(mesh):
    return jax.shard_map(
        body,
        mesh=mesh,
        in_specs=(P("win", "chan", None), P("win"), P()),
        out_specs=P(None, "win", None, "chan"),
        check_vma=False,
    )
```

profile of v0, /device:TPU:1, one launch (start us, length us, event | category | flops | bytes accessed | tf_op | source)
XLA Modules:
  0.0 912.9 jit_solution(7509208013079478190)
XLA Ops:
  6.5 24.8 %copy.27 = bf16[3,248,8192]{1,0,2:T(4,128)(2,1)} copy(bf16[3,248,8192]{2,1,0:T(8,128)(2,1)} %param.3) | data formatting | bytes 24379392 | tf_op args[0]
  31.4 9.5 %all-to-all-start = ((bf16[3,248,8192]{1,0,2:T(4,128)(2,1)}), bf16[3,248,8192]{1,0,2:T(4,128)(2,1)}, u32[]{:S(2)}, u32[]{:S(2)}) async-start(bf16[3,248,8192]{1,0,2:T(4,128)(2,1)} %copy.27), calls=%async_computation | async-start | bytes 33554432 | tf_op jit(solution)/shard_map/all_to_all | solution.py:61
  40.9 0.7 fusion.48
  47.5 0.1 multiply_subtract_fusion
  47.7 33.9 %multiply_convert_fusion.1 = (bf16[256,7680]{1,0:T(8,128)(2,1)}, bf16[256,7680]{1,0:T(8,128)(2,1)}) fusion(s32[256]{0:T(256)S(1)} %get-tuple-element.39, f32[7680]{0:T(1024)S(1)} %get-tuple-element.37, f32[7680]{0:T(1024)S(1)} %get-tuple-element.38), kind=kLoop, calls=%fused_computation.17 | loop fusion | flops 25559040 | bytes 7926784 | tf_op jit(solution)/shard_map/convert.24
  81.6 265.3 %all-to-all-done = bf16[3,248,8192]{1,0,2:T(4,128)(2,1)} async-done(((bf16[3,248,8192]{1,0,2:T(4,128)(2,1)}), bf16[3,248,8192]{1,0,2:T(4,128)(2,1)}, u32[]{:S(2)}, u32[]{:S(2)}) %all-to-all-start) | async-done | bytes 12189728 | tf_op jit(solution)/shard_map/all_to_all | solution.py:61
  346.8 18.7 %copy.38 = bf16[3,248,32,256]{3,2,1,0:T(8,128)(2,1)} copy(bf16[3,248,32,256]{1,0,3,2:T(4,128)(2,1)} %bitcast.3) | data formatting | bytes 24379392 | tf_op jit(solution)/shard_map/all_to_all | solution.py:61
  365.5 5.4 fusion.47
  370.9 2.3 copy.29
  373.3 2.3 copy.31
  375.7 2.3 copy.30
  378.0 2.2 fusion.14
  380.3 2.2 fusion.20
  382.5 2.5 fusion.17
  385.0 0.1 multiply_reduce_fusion
  385.1 0.2 multiply_convert_fusion.2
  385.3 0.9 fusion.25
  386.3 0.9 fusion.24
  387.2 0.9 fusion.23
  388.2 1.9 cosine_bitcast_fusion
  390.1 292.5 %all-reduce.3.cloned.1.call-done = (bf16[3,512,16]{1,2,0:T(8,128)(2,1)}, bf16[3,512,16]{1,2,0:T(8,128)(2,1)}, bf16[3,512,16]{1,2,0:T(8,128)(2,1)}) async-done(((bf16[3,512,16]{1,2,0:T(8,128)(2,1)}, bf16[3,512,16]{1,2,0:T(8,128)(2,1)}, bf16[3,512,16]{1,2,0:T(8,128)(2,1)}), (bf16[3,512,16]{1,2,0:T(8,128)(2,1)}, bf16[3,512,16]{1,2,0:T(8,128)(2,1)}, bf16[3,512,16]{1,2,0:T(8,128)(2,1)})) %all-reduce.3.cloned.1.call-update) | async-done | bytes 147472 | tf_op jit(solution)/shard_map/psum | solution.py:78
  682.7 0.8 convert_bitcast_fusion.1
  683.4 0.8 convert_bitcast_fusion.3
  684.2 0.8 convert_bitcast_fusion.5
  685.0 0.2 copy.32
  685.1 0.2 copy.34
  685.3 0.2 copy.36
  685.5 0.2 copy.33
  685.6 0.2 copy.35
  685.8 0.2 copy.37
  686.0 24.9 %add_bitcast_fusion.2 = (f32[16,256,3,256]{1,0,3,2:T(8,128)}, f32[16,256,3,256]{1,0,3,2:T(8,128)}, f32[16,256,3,256]{1,0,3,2:T(8,128)}, f32[16,256,3,256]{1,0,3,...) fusion(f32[256,3,16]{2,0,1:T(8,128)S(1)} %copy.33, f32[256,256]{1,0:T(8,128)} %get-tuple-element.28, ...), kind=kLoop, calls=%fused_computation.11 | loop fusion | flops 56623104 | bytes 76316672 | tf_op jit(solution)/shard_map/add | solution.py:42
  710.9 9.7 %fusion = bf16[16,256,3,512]{1,0,3,2:T(8,128)(2,1)S(1)} fusion(f32[16,256,3,256]{1,0,3,2:T(8,128)} %get-tuple-element.12, f32[16,256,3,256]{1,0,3,2:T(8,128)} %get-tuple-element.11), kind=kLoop, calls=%fused_computation.1 | loop fusion | flops 18874368 | bytes 37748736 | tf_op jit(solution)/shard_map/convert_element_type | solution.py:50
  720.7 4.8 copy.39
  725.5 5.4 fusion.49
  731.0 0.0 reduce-scatter.6.cloned.1.call-start
  731.0 9.7 %fusion.1 = bf16[16,256,3,512]{1,0,3,2:T(8,128)(2,1)S(1)} fusion(f32[16,256,3,256]{1,0,3,2:T(8,128)} %get-tuple-element.17, f32[16,256,3,256]{1,0,3,2:T(8,128)} %get-tuple-element.18), kind=kLoop, calls=%fused_computation.3 | loop fusion | flops 18874368 | bytes 37748736 | tf_op jit(solution)/shard_map/convert_element_type | solution.py:50
  740.8 4.8 copy.40
  745.6 5.4 fusion.50
  751.1 11.2 %fusion.2 = bf16[16,256,3,512]{1,0,3,2:T(8,128)(2,1)S(1)} fusion(f32[16,256,3,256]{1,0,3,2:T(8,128)} %get-tuple-element.19, f32[16,256,3,256]{1,0,3,2:T(8,128)} %get-tuple-element.20), kind=kLoop, calls=%fused_computation.5 | loop fusion | flops 18874368 | bytes 37748736 | tf_op jit(solution)/shard_map/convert_element_type | solution.py:50
  762.3 4.8 copy.41
  767.1 5.3 fusion.51
  772.5 24.3 %reduce-scatter.4.cloned.1.call-done = f32[1024,256]{1,0:T(8,128)} async-done(((f32[4096,256]{1,0:T(8,128)}), f32[1024,256]{1,0:T(8,128)}) %reduce-scatter.4.cloned.1.call-update) | async-done | bytes 1048592 | tf_op jit(solution)/shard_map/reduce_scatter | solution.py:84
  796.9 1.3 convert_element_type.144
  798.1 52.1 %reduce-scatter.6.cloned.1.call-done = f32[1024,256]{1,0:T(8,128)} async-done(((f32[4096,256]{1,0:T(8,128)}), f32[1024,256]{1,0:T(8,128)}) %reduce-scatter.6.cloned.1.call-update) | async-done | bytes 1048592 | tf_op jit(solution)/shard_map/reduce_scatter | solution.py:84
  850.3 1.3 convert_element_type.151
  851.6 52.2 %reduce-scatter.8.cloned.1.call-done = f32[1024,256]{1,0:T(8,128)} async-done(((f32[4096,256]{1,0:T(8,128)}), f32[1024,256]{1,0:T(8,128)}) %reduce-scatter.8.cloned.1.call-update) | async-done | bytes 1048592 | tf_op jit(solution)/shard_map/reduce_scatter | solution.py:84
  903.8 1.3 convert_element_type.158
  905.1 1.3 pad_maximum_fusion.5
  (18 shorter events, 0.2 us)
Async XLA Ops:
  31.4 9.6 %copy-start.2 = (s32[3]{0:T(128)S(1)}, s32[3]{0:T(128)}, u32[]{:S(2)}) copy-start(s32[3]{0:T(128)} %param.4) | copy-start | bytes 40
  31.4 16.3 %copy-start.3 = (s32[3,16]{1,0:T(4,128)S(1)}, s32[3,16]{1,0:T(4,128)}, u32[]{:S(2)}) copy-start(s32[3,16]{1,0:T(4,128)} %param.5) | copy-start | bytes 580
  31.4 315.5 %all-to-all-start = ((bf16[3,248,8192]{1,0,2:T(4,128)(2,1)}), bf16[3,248,8192]{1,0,2:T(4,128)(2,1)}, u32[]{:S(2)}, u32[]{:S(2)}) async-start(bf16[3,248,8192]{1,0,2:T(4,128)(2,1)} %copy.27), calls=%async_computation | async-start | bytes 33554432 | tf_op jit(solution)/shard_map/all_to_all | solution.py:61
  40.9 641.8 %all-reduce.3.cloned.1.call-start = ((), (), s32[]{:S(2)}) async-start(), calls=%async_computation.7 | async-start | bytes 294912 | tf_op jit(solution)/shard_map/psum | solution.py:78
  373.3 4.7 copy-start
  373.3 4.7 copy-start.1
  388.2 408.7 %reduce-scatter.4.cloned.1.call-start = ((), (), s32[]{:S(2)}) async-start(), calls=%async_computation.4 | async-start | bytes 5242880 | tf_op jit(solution)/shard_map/reduce_scatter | solution.py:84
  731.0 119.3 %reduce-scatter.6.cloned.1.call-start = ((), (), s32[]{:S(2)}) async-start(), calls=%async_computation.5 | async-start | bytes 5242880 | tf_op jit(solution)/shard_map/reduce_scatter | solution.py:84
  751.0 152.8 %reduce-scatter.8.cloned.1.call-start = ((), (), s32[]{:S(2)}) async-start(), calls=%async_computation.6 | async-start | bytes 5242880 | tf_op jit(solution)/shard_map/reduce_scatter | solution.py:84
Sparse Core Ops, SparseCore 0:
  388.3 294.3 all-reduce.2
  731.1 65.7 reduce-scatter.3
  799.5 50.7 reduce-scatter.5
  853.0 50.7 reduce-scatter.7
where the time goes:
time: 915 us; the launch traced here: 913 us
  waiting for transfers between devices  687 us (75%)
  other arithmetic  99.4 us (11%)
  local copies, waits for them, and re-layouts  72.1 us (8%)
  matrix products  25.9 us (3%)
  between operations  19.2 us (2%)
  starting transfers between devices  9.65 us (1%)
    psum x1, waiting for transfers between devices, body(): lax.psum(select_columns(white, sources[step:step + 1], first_channel)[0]....  293 us
    all_to_all x1, waiting for transfers between devices, body(): lax.all_to_all(record, 'chan', split_axis=2, concat_axis=1, tiled=True)  265 us
    reduce_scatter x3, waiting for transfers between devices, body(): share = lax.psum_scatter(joint, 'win', scatter_dimension=0, tiled=True)  129 us
    unnamed x12, local copies, waits for them, and re-layouts  39.3 us
    another operation x4, other arithmetic  36.2 us
    convert_element_type x3, other arithmetic, make_kernel(): joined.reshape(count * LAGS, chosen.shape[0] * 2 * BINS)  30.7 us
    add x1, other arithmetic, make_kernel(): jnp.einsum('wfs,kf->skwf', real_part, cos_lag, precision=high)  24.9 us
    all_to_all x1, local copies, waits for them, and re-layouts, body(): lax.all_to_all(record, 'chan', split_axis=2, concat_axis=1, tiled=True)  18.7 us
  transfers between devices with their start and end apart: 5, of which 5 were waited for; matrix products, arithmetic and copies ran while one was open for 9% of the time, Pallas kernels for 0%

commit v1 on v0

v1 whole, which is shorter than its diff:
```python
import math

import jax
import jax.numpy as jnp
import numpy as np
from jax import lax
from jax.sharding import PartitionSpec as P

SAMPLES = 7680
BINS = 256
F0 = 16
LAGS = 256
LAG_STEP = 8
ROUNDS = 3
RANK = 32
GROUPS = BINS // 8
SLOTS = 16


def sample_basis(count):
    half = (F0 + BINS) / SAMPLES
    at = np.arange(count)
    matrix = np.diag(((count - 1) / 2 - at) ** 2 * math.cos(2 * math.pi * half))
    side = at[1:] * (count - at[1:]) / 2
    matrix = matrix + np.diag(side, 1) + np.diag(side, -1)
    vectors = np.linalg.eigh(matrix)[1][:, ::-1][:, :RANK]
    return vectors * np.where(vectors[0] < 0, -1.0, 1.0)


def spectrum_tables(count, blocks):
    basis = sample_basis(count)
    middle = (count - 1) / 2
    at = np.arange(count) - middle
    terms = []
    for step, weight in ((0, 0.5), (1, -0.25), (-1, -0.25)):
        freqs = np.arange(BINS) + F0 + step
        wave = np.exp(-2j * math.pi / SAMPLES * np.outer(freqs, at)) @ basis
        turn = np.exp(-2j * math.pi / SAMPLES * np.outer(freqs, count * np.arange(blocks) + middle))
        terms.append(weight * (turn[:, :, None] * wave[:, None, :]).reshape(BINS, blocks * RANK))
    own, above, below = terms
    return np.stack([np.stack([t.real, t.imag]) for t in (own, above + below, above - below)]).astype(np.float32)


def lag_matrix(scale):
    shifts = LAG_STEP * (np.arange(LAGS) - LAGS // 2)
    phase = shifts[:, None] * (np.arange(BINS) + F0)[None, :] % SAMPLES
    angle = 2 * math.pi / SAMPLES * phase
    both = np.stack([np.cos(angle), np.sin(angle)], axis=1).reshape(LAGS, 2, GROUPS, 8)
    return (both.transpose(0, 2, 1, 3).reshape(LAGS, 2 * BINS) * scale).astype(np.float32)


def split_pair(array):
    high = array.astype(jnp.bfloat16)
    return high, (array - high.astype(jnp.float32)).astype(jnp.bfloat16)


def body(record, offsets, sources):
    windows, count, channels = record.shape
    blocks, hosts = lax.axis_size("chan"), lax.axis_size("win")
    width = channels // blocks
    first = lax.axis_index("chan") * count

    at = first + jnp.arange(count, dtype=jnp.int32)[None, :] - offsets[:, None]
    inside = (at >= 0) & (at < SAMPLES)
    basis = jnp.asarray(sample_basis(count).T.astype(np.float32))
    masked = jnp.where(inside[:, None, :], basis[None], 0.0)
    high, low = split_pair(masked)
    pair = jnp.concatenate([high, low], axis=1)
    coef = jnp.einsum("wrj,wjc->wrc", pair, record, preferred_element_type=jnp.float32)
    coef = (coef[:, :RANK] + coef[:, RANK:]).astype(jnp.bfloat16)

    per = sources.shape[1] // hosts
    wanted = sources.reshape(ROUNDS, hosts, per).transpose(1, 0, 2).reshape(hosts, ROUNDS * per)
    wanted = jnp.pad(wanted, ((0, 0), (0, SLOTS - ROUNDS * per)), constant_values=-1).reshape(-1)
    onehot = (jnp.arange(channels, dtype=jnp.int32)[:, None] == wanted[None, :]).astype(jnp.bfloat16)
    picked = jnp.einsum("wrc,cs->wrs", coef, onehot, preferred_element_type=jnp.float32).astype(jnp.bfloat16)

    cut = coef.reshape(windows, RANK, blocks, width).transpose(2, 0, 1, 3)
    extra = jnp.broadcast_to(picked[None], (blocks,) + picked.shape)
    sent = jnp.concatenate([cut, extra], axis=3)
    got = lax.all_to_all(sent, "chan", split_axis=0, concat_axis=0, tiled=True)
    got = got.transpose(1, 0, 2, 3).reshape(windows, blocks * RANK, -1)

    tables = jnp.asarray(spectrum_tables(count, blocks))
    freqs = jnp.arange(BINS, dtype=jnp.int32) + F0
    turn = 2 * math.pi / SAMPLES * (freqs[None, :] * offsets[:, None] % SAMPLES).astype(jnp.float32)
    step = 2 * math.pi / SAMPLES * offsets.astype(jnp.float32)
    white = []
    for w in range(windows):
        c, s = jnp.cos(step[w]), jnp.sin(step[w])
        re = tables[0, 0] + c * tables[1, 0] - s * tables[2, 1]
        im = tables[0, 1] + c * tables[1, 1] + s * tables[2, 0]
        c, s = jnp.cos(turn[w])[:, None], jnp.sin(turn[w])[:, None]
        full = jnp.stack([(c * re - s * im).reshape(GROUPS, 8, -1), (c * im + s * re).reshape(GROUPS, 8, -1)], axis=1)
        full = full.reshape(2 * BINS, -1).astype(jnp.bfloat16)
        spectra = jnp.dot(full, got[w], preferred_element_type=jnp.float32)
        power = jnp.mean(spectra * spectra, axis=0, keepdims=True)
        white.append((spectra * lax.rsqrt(power + 1e-06)).astype(jnp.bfloat16))
    white = jnp.stack(white)
    white = lax.all_gather(white, "win", axis=0, tiled=True)
    mine = lax.dynamic_slice_in_dim(white, width + SLOTS * lax.axis_index("win"), ROUNDS * per, 2)
    white = white[:, :, :width]

    total = windows * hosts
    count = ROUNDS * per
    white = white.reshape(total, GROUPS, 16, width).transpose(1, 0, 2, 3).reshape(GROUPS, total * 16, width)
    mine = mine.reshape(total, GROUPS, 2, 8, count)
    turned = jnp.stack([mine[:, :, 1], -mine[:, :, 0]], axis=2)
    rows = jnp.stack([mine, turned]).transpose(2, 5, 0, 1, 3, 4)
    eye = jnp.eye(8, dtype=jnp.bfloat16)
    spread = (rows[:, :, :, None] * eye[:, None, None, :]).reshape(GROUPS, count * 16, total * 16)
    cross = jnp.einsum("gmk,gkc->gmc", spread, white, preferred_element_type=jnp.float32).astype(jnp.bfloat16)
    cross = cross.reshape(GROUPS, count, 16, width).transpose(1, 0, 2, 3).reshape(count, 2 * BINS, width)
    lags = jnp.asarray(lag_matrix(1 / math.sqrt(total * BINS))).astype(jnp.bfloat16)
    out = jnp.einsum("kf,sfc->skc", lags, cross, preferred_element_type=jnp.float32)
    return out.astype(jnp.bfloat16).reshape(ROUNDS, per, LAGS, width)


def solution(mesh):
    return jax.shard_map(
        body,
        mesh=mesh,
        in_specs=(P("win", "chan", None), P("win"), P()),
        out_specs=P(None, "win", None, "chan"),
        check_vma=False,
    )
```

time: 915 us -> 177 us (0.19)
  waiting for transfers between devices: 687 us -> 56.1 us
  other arithmetic: 99.4 us -> 18.2 us
  matrix products: 25.9 us -> 13.6 us
  local copies, waits for them, and re-layouts: 72.1 us -> 61.1 us
    psum x1 -> x0, waiting for transfers between devices: 293 us -> none  [body(): lax.psum(select_columns(white, sources[step:step + 1], first_channel)[0]....]
    all_to_all x1, waiting for transfers between devices: 265 us -> 19 us  [body(): got = lax.all_to_all(sent, 'chan', split_axis=0, concat_axis=0, tiled=True)]
    reduce_scatter x3 -> x0, waiting for transfers between devices: 129 us -> none  [body(): share = lax.psum_scatter(joint, 'win', scatter_dimension=0, tiled=True)]
    all_gather x0 -> x1, waiting for transfers between devices: none -> 37 us  [body(): white = lax.all_gather(white, 'win', axis=0, tiled=True)]
    convert_element_type x7 -> x4, other arithmetic: 34.7 us -> 1.85 us  [the longest x1 0.77 us: split_pair(): high = array.astype(jnp.bfloat16)]
    unnamed x12 -> x18, local copies, waits for them, and re-layouts: 39.3 us -> 7.77 us
    another operation x5 -> x8, other arithmetic: 37.5 us -> 6.52 us
    add x2, other arithmetic: 24.9 us -> 0.01 us  [the longest x1 0.01 us: body(): freqs = jnp.arange(BINS, dtype=jnp.int32) + F0]
  transfers between devices with their start and end apart: 5 -> 2, of which waited for: 5 -> 2; matrix products, arithmetic and copies ran while one was open for 9% -> 5% of each run, Pallas kernels for 0% -> 0%
where the time goes in v1:
time: 177 us; the launch traced here: 176 us
  local copies, waits for them, and re-layouts  61.1 us (35%)
  waiting for transfers between devices  56.1 us (32%)
  other arithmetic  18.2 us (10%)
  between operations  17.9 us (10%)
  matrix products  13.6 us (8%)
  starting transfers between devices  9.58 us (5%)
    all_gather x1, waiting for transfers between devices, body(): white = lax.all_gather(white, 'win', axis=0, tiled=True)  37 us
    all_to_all x1, waiting for transfers between devices, body(): got = lax.all_to_all(sent, 'chan', split_axis=0, concat_axis=0, tiled=True)  19 us
    mul x4, local copies, waits for them, and re-layouts, body(): rows[:, :, :, None] * eye[:, None, None, :]  14.3 us
    slice x2, local copies, waits for them, and re-layouts, body(): turned = jnp.stack([mine[:, :, 1], -mine[:, :, 0]], axis=2)  13.8 us
    all_to_all x1, starting transfers between devices, body(): got = lax.all_to_all(sent, 'chan', split_axis=0, concat_axis=0, tiled=True)  9.36 us
    another operation x2, local copies, waits for them, and re-layouts, body(): rows = jnp.stack([mine, turned]).transpose(2, 5, 0, 1, 3, 4)  8.69 us
    unnamed x18, local copies, waits for them, and re-layouts  7.77 us
    dot_general x1, matrix products, body(): jnp.einsum('wrj,wjc->wrc', pair, record, preferred_element_type=jnp.float32)  7.05 us
  transfers between devices with their start and end apart: 2, of which 2 were waited for; matrix products, arithmetic and copies ran while one was open for 5% of the time, Pallas kernels for 0%

profile of v1, /device:TPU:1, one launch (start us, length us, event | category | flops | bytes accessed | tf_op | source)
XLA Modules:
  0.0 176.4 jit_solution(17351235663465805740)
XLA Ops:
  6.5 0.7 fusion.33
  7.3 0.8 fusion.23
  8.0 0.8 select_convert_fusion
  8.8 0.8 reshape.618
  9.8 7.1 %fusion.24 = f32[3,64,8192]{2,1,0:T(8,128)S(1)} fusion(bf16[3,248,8192]{2,1,0:T(8,128)(2,1)} %param.6, bf16[3,32,248]{2,1,0:T(8,128)(2,1)S(1)} %fusion.23, bf16[3,32,248]{2,1,0:T(8,128)(2,1)S(1)} %select_convert_fusion), kind=kOutput, calls=%fused_computation.60 | convolution fusion | flops 780331008 | bytes 18576384 | tf_op jit(solution)/shard_map/wrj,wjc->wrc/dot_general | solution.py:69
  16.8 0.3 fusion
  17.1 0.6 fusion.4
  17.8 0.2 copy.59
  18.1 1.8 %pad_maximum_fusion = bf16[32,3,32,320]{3,2,1,0:T(8,128)(2,1)} fusion(bf16[32,3,32,64]{3,2,1,0:T(8,128)(2,1)S(1)} %broadcast_in_dim.25, bf16[32,3,32,256]{3,2,1,0:T(8,128)(2,1)S(1)} %bitcast.126), kind=kLoop, calls=%fused_computation.3 | loop fusion | flops 3932160 | bytes 3932160 | tf_op jit(solution)/shard_map/concatenate | solution.py:80
  19.9 9.4 %all-to-all-start = ((bf16[32,3,32,320]{3,2,1,0:T(8,128)(2,1)}), bf16[32,3,32,320]{3,2,1,0:T(8,128)(2,1)S(1)}, u32[]{:S(2)}, u32[]{:S(2)}) async-start(bf16[32,3,32,320]{3,2,1,0:T(8,128)(2,1)} %pad_maximum_fusion), calls=%async_computation | async-start | bytes 4718592 | tf_op jit(solution)/shard_map/all_to_all | solution.py:81
  29.2 0.2 all-gather.2.cloned.1.call-start
  29.5 0.7 fusion.38
  34.5 0.1 cosine_reduce_fusion.2
  35.2 3.4 %fusion.16 = (bf16[32,1,8,1024]{3,2,1,0:T(8,128)(2,1)S(1)}, bf16[32,1,8,1024]{3,2,1,0:T(8,128)(2,1)S(1)}, bf16[32,1,8,1024]{3,2,1,0:T(8,128)(2,1)S(1)}, bf16[32,...) fusion(f32[1,1,256,1024]{3,2,1,0:T(8,128)S(1)} %copy-done.4, ...), kind=kLoop, calls=%fused_computation.34 | loop fusion | flops 12582912 | bytes 9443352 | tf_op jit(solution)/shard_map/convert.4
  38.7 1.5 pad_maximum_fusion.1
  40.2 19.0 %all-to-all-done = bf16[32,3,32,320]{3,2,1,0:T(8,128)(2,1)S(1)} async-done(((bf16[32,3,32,320]{3,2,1,0:T(8,128)(2,1)}), bf16[32,3,32,320]{3,2,1,0:T(8,128)(2,1)S(1)}, u32[]{:S(2)}, u32[]{:S(2)}) %all-to-all-start) | async-done | bytes 1966112 | tf_op jit(solution)/shard_map/all_to_all | solution.py:81
  59.2 0.3 fusion.37
  59.5 0.9 copy-done.3
  60.5 0.7 multiply_reduce_fusion.1
  61.1 0.7 multiply_reduce_fusion.2
  61.8 0.7 multiply_reduce_fusion
  62.5 0.1 fusion.21
  62.6 0.1 fusion.20
  62.8 1.1 pad_maximum_fusion.4
  63.9 1.0 mul.508
  64.9 1.4 mul.509
  66.3 37.0 %all-gather.2.cloned.1.call-done = bf16[12,512,320]{1,2,0:T(8,128)(2,1)} async-done(((bf16[3,512,320]{1,2,0:T(8,128)(2,1)}), bf16[12,512,320]{1,2,0:T(8,128)(2,1)}) %all-gather.2.cloned.1.call-update) | async-done | bytes 3932176 | tf_op jit(solution)/shard_map/all_gather | solution.py:100
  103.3 1.0 constant_dynamic-slice_fusion
  104.4 2.8 %reshape.620 = bf16[12,32,2,8,12]{3,2,1,4,0:T(2,128)(2,1)S(1)} reshape(bf16[12,512,12]{1,2,0:T(8,128)(2,1)S(1)} %constant_dynamic-slice_fusion) | data formatting | bytes 294912 | tf_op jit(solution)/shard_map/reshape | solution.py:107
  107.1 3.9 %stack_reshape.2 = bf16[1,12,32,2,8,12]{4,3,2,5,1,0:T(2,128)(2,1)} reshape(bf16[12,512,12]{1,2,0:T(8,128)(2,1)S(1)} %constant_dynamic-slice_fusion) | data formatting | bytes 294912 | tf_op jit(solution)/shard_map/stack;reshape | solution.py:109
  111.0 3.8 %slice.111 = bf16[12,512,256]{1,2,0:T(8,128)(2,1)} slice(bf16[12,512,320]{1,2,0:T(8,128)(2,1)} %all-gather.2.cloned.1.call-done), slice={[0:12], [0:512], [0:256]} | slice | bytes 6291456 | tf_op jit(solution)/shard_map/slice | solution.py:102
  114.8 4.6 %copy.56 = bf16[12,512,256]{2,1,0:T(8,128)(2,1)} copy(bf16[12,512,256]{1,2,0:T(8,128)(2,1)} %slice.111) | data formatting | bytes 6291456
  119.4 3.9 %copy.49 = bf16[32,12,16,256]{3,2,1,0:T(8,128)(2,1)} copy(bf16[32,12,16,256]{3,2,0,1:T(8,128)(2,1)} %bitcast.121) | data formatting | bytes 6291456 | tf_op jit(solution)/shard_map/transpose | solution.py:106
  123.4 4.8 %copy.46 = bf16[1,12,32,2,8,12]{2,4,5,3,1,0:T(8,128)(2,1)S(1)} copy(bf16[1,12,32,2,8,12]{4,3,2,5,1,0:T(2,128)(2,1)} %stack_reshape.2) | data formatting | bytes 294912 | tf_op jit(solution)/shard_map/stack;reshape | solution.py:109
  128.2 9.0 %fusion.36 = (bf16[12,32,1,8,12]{3,2,1,4,0:T(2,128)(2,1)}, bf16[12,32,1,8,12]{3,2,1,4,0:T(2,128)(2,1)}) fusion(bf16[12,32,2,8,12]{3,2,1,4,0:T(2,128)(2,1)S(1)} %reshape.620), kind=kLoop, calls=%fused_computation.90 | loop fusion | bytes 294912 | tf_op jit(solution)/shard_map/slice | solution.py:108
  137.2 4.8 %copy.45 = bf16[12,32,1,8,12]{1,3,4,2,0:T(8,128)(2,1)S(1)} copy(bf16[12,32,1,8,12]{3,2,1,4,0:T(2,128)(2,1)} %get-tuple-element.21) | data formatting | bytes 147456 | tf_op jit(solution)/shard_map/slice | solution.py:108
  142.0 1.5 copy.55
  143.6 0.1 maximum_bitcast_fusion.1
  143.7 0.3 maximum_bitcast_fusion
  144.0 0.3 copy.47
  144.3 2.4 %mul.506 = bf16[32,12,2,8,12,2,8]{0,6,5,4,3,2,1:T(8,128)(2,1)S(1)} broadcast(bf16[32,12,2,12,2,8]{0,5,4,3,2,1:T(8,128)(2,1)S(1)} %copy.47), dimensions={0,1,2,4,5,6} | broadcast | bytes 2654208 | tf_op jit(solution)/shard_map/mul | solution.py:111
  146.7 6.9 %broadcast_multiply_fusion = bf16[32,192,192]{0,2,1:T(8,128)(2,1)} fusion(bf16[32,192,192]{0,2,1:T(8,128)(2,1)S(1)} %bitcast.119, bf16[192,192]{1,0:T(8,128)(2,1)S(1)} %copy-done.5), kind=kLoop, calls=%fused_computation | loop fusion | flops 1179648 | bytes 4792320 | tf_op jit(solution)/shard_map/mul | solution.py:111
  153.6 9.6 %copy.50 = bf16[32,192,192]{2,1,0:T(8,128)(2,1)} copy(bf16[32,192,192]{0,2,1:T(8,128)(2,1)} %broadcast_multiply_fusion) | data formatting | bytes 4718592 | tf_op jit(solution)/shard_map/mul | solution.py:111
  163.2 2.9 %convolution_convert_fusion = bf16[32,192,256]{2,1,0:T(8,128)(2,1)S(1)} fusion(bf16[32,192,192]{2,1,0:T(8,128)(2,1)} %copy.50, bf16[32,192,256]{2,1,0:T(8,128)(2,1)S(1)} %bitcast.122), kind=kOutput, calls=%fused_computation.4 | convolution fusion | flops 605552640 | bytes 8650752 | tf_op jit(solution)/shard_map/gmk,gkc->gmc/dot_general | solution.py:112
  166.0 0.3 copy.51
  166.4 0.6 copy-done.6
  167.0 1.0 convolution_convert_fusion.1
  168.0 1.6 copy.53
  (37 shorter events, 1.3 us)
Async XLA Ops:
  19.9 9.6 %copy-start.7 = (s32[3]{0:T(128)S(1)}, s32[3]{0:T(128)}, u32[]{:S(2)}) copy-start(s32[3]{0:T(128)} %param.7) | copy-start | bytes 40
  19.9 15.3 %copy-start.4 = (f32[1,1,256,1024]{3,2,1,0:T(8,128)S(1)}, f32[1,1,256,1024]{3,2,1,0:T(8,128)}, u32[]{:S(2)}) copy-start(f32[1,1,256,1024]{3,2,1,0:T(8,128)} %constant.66) | copy-start | bytes 3145732
  19.9 39.3 %all-to-all-start = ((bf16[32,3,32,320]{3,2,1,0:T(8,128)(2,1)}), bf16[32,3,32,320]{3,2,1,0:T(8,128)(2,1)S(1)}, u32[]{:S(2)}, u32[]{:S(2)}) async-start(bf16[32,3,32,320]{3,2,1,0:T(8,128)(2,1)} %pad_maximum_fusion), calls=%async_computation | async-start | bytes 4718592 | tf_op jit(solution)/shard_map/all_to_all | solution.py:81
  29.2 74.1 %all-gather.2.cloned.1.call-start = ((), (), s32[]{:S(2)}) async-start(), calls=%async_computation.1 | async-start | bytes 4915200 | tf_op jit(solution)/shard_map/all_gather | solution.py:100
  59.2 1.2 copy-start.3
  59.2 1.9 %copy-start.2 = (bf16[32,2,8,1024]{3,2,1,0:T(8,128)(2,1)S(1)}, bf16[32,2,8,1024]{3,2,1,0:T(8,128)(2,1)}, u32[]{:S(2)}) copy-start(bf16[32,2,8,1024]{3,2,1,0:T(8,128)(2,1)} %get-tuple-element.35) | copy-start | bytes 3145732
  137.2 4.8 %copy-start.1 = (bf16[12,32,1,8,12]{3,2,1,4,0:T(2,128)(2,1)S(1)}, bf16[12,32,1,8,12]{3,2,1,4,0:T(2,128)(2,1)}, u32[]{:S(2)}) copy-start(bf16[12,32,1,8,12]{3,2,1,4,0:T(2,128)(2,1)} %get-tuple-element.22) | copy-start | bytes 221188
  144.3 2.4 %copy-start.5 = (bf16[192,192]{1,0:T(8,128)(2,1)S(1)}, bf16[192,192]{1,0:T(8,128)(2,1)}, u32[]{:S(2)}) copy-start(bf16[192,192]{1,0:T(8,128)(2,1)} %mul.509) | copy-start | bytes 221188
  153.6 9.6 %copy-start = (bf16[32,12,16,256]{3,2,1,0:T(8,128)(2,1)S(1)}, bf16[32,12,16,256]{3,2,1,0:T(8,128)(2,1)}, u32[]{:S(2)}) copy-start(bf16[32,12,16,256]{3,2,1,0:T(8,128)(2,1)} %copy.49) | copy-start | bytes 9437188
  166.0 1.0 copy-start.6
Sparse Core Ops, SparseCore 0:
  64.0 39.2 all-gather.1

commit v2 on v1

--- a/solution.py
+++ b/solution.py
@@ -4,6 +4,8 @@
 import jax.numpy as jnp
 import numpy as np
 from jax import lax
+from jax.experimental import pallas as pl
+from jax.experimental.pallas import tpu as pltpu
 from jax.sharding import PartitionSpec as P
 
 SAMPLES = 7680
@@ -54,6 +56,67 @@
     return high, (array - high.astype(jnp.float32)).astype(jnp.bfloat16)
 
 
+def correlate(white_ref, rows_ref, lag_ref, out_ref, cross):
+    hosts, windows = white_ref.shape[:2]
+    used = cross.shape[0]
+
+    @pl.when(pl.program_id(0) == 0)
+    def _():
+        lane = lax.broadcasted_iota(jnp.int32, (SLOTS, 128), 1)
+        left = lane < 64
+        real = lane % 16 < 8
+        own = lax.broadcasted_iota(jnp.int32, (8, 256), 1) % 8 == lax.broadcasted_iota(jnp.int32, (8, 256), 0)
+        own = jnp.where(own, 1.0, 0.0).astype(jnp.float32)
+        blank = jnp.zeros((16, white_ref.shape[4]), jnp.bfloat16)
+
+        def pair(at, _):
+            tiles = [rows_ref[j, at].astype(jnp.float32) for j in range(hosts)]
+            for odd in range(2):
+                halves, turned = [], []
+                for j in range(0, hosts, 2):
+                    if odd:
+                        both = jnp.where(left, pltpu.roll(tiles[j], 64, 1), tiles[j + 1])
+                    else:
+                        both = jnp.where(left, tiles[j], pltpu.roll(tiles[j + 1], 64, 1))
+                    halves.append(both)
+                    turned.append(jnp.where(real, pltpu.roll(both, 120, 1), -pltpu.roll(both, 8, 1)))
+                first = jnp.concatenate(halves, axis=1)[:used]
+                second = jnp.concatenate(turned, axis=1)[:used]
+                spread = jnp.stack([first[:, None, :] * own[None], second[:, None, :] * own[None]], axis=1)
+                spread = spread.reshape(used * 16, 256).astype(jnp.bfloat16)
+                group = at * 2 + odd
+                parts = []
+                for j in range(hosts):
+                    parts += [white_ref[j, w, group] for w in range(windows)] + [blank]
+                found = jnp.dot(spread, jnp.concatenate(parts, axis=0), preferred_element_type=jnp.float32)
+                cross[:, group] = found.astype(jnp.bfloat16).reshape(used, 16, -1)
+            return 0
+
+        lax.fori_loop(0, GROUPS // 2, pair, 0)
+
+    spectrum = cross[pl.program_id(0)].reshape(2 * BINS, -1)
+    found = jnp.dot(lag_ref[...], spectrum, preferred_element_type=jnp.float32)
+    out_ref[0] = (found[:LAGS] + found[LAGS:]).astype(jnp.bfloat16)
+
+
+def correlations(white, rows, total, used):
+    hosts, windows, _, _, width = white.shape
+    lags = split_pair(jnp.asarray(lag_matrix(1 / math.sqrt(total * BINS))))
+    return pl.pallas_call(
+        correlate,
+        grid=(used,),
+        out_shape=jax.ShapeDtypeStruct((used, LAGS, width), jnp.bfloat16),
+        in_specs=[
+            pl.BlockSpec(white.shape, lambda s: (0,) * 5),
+            pl.BlockSpec(rows.shape, lambda s: (0,) * 4),
+            pl.BlockSpec((2 * LAGS, 2 * BINS), lambda s: (0, 0)),
+        ],
+        out_specs=pl.BlockSpec((1, LAGS, width), lambda s: (s, 0, 0)),
+        scratch_shapes=[pltpu.VMEM((used, GROUPS, 16, width), jnp.bfloat16)],
+        compiler_params=pltpu.CompilerParams(vmem_limit_bytes=32 << 20),
+    )(white, rows, jnp.concatenate(lags, axis=0))
+
+
 def body(record, offsets, sources):
     windows, count, channels = record.shape
     blocks, hosts = lax.axis_size("chan"), lax.axis_size("win")
@@ -97,23 +160,14 @@
         power = jnp.mean(spectra * spectra, axis=0, keepdims=True)
         white.append((spectra * lax.rsqrt(power + 1e-06)).astype(jnp.bfloat16))
     white = jnp.stack(white)
-    white = lax.all_gather(white, "win", axis=0, tiled=True)
-    mine = lax.dynamic_slice_in_dim(white, width + SLOTS * lax.axis_index("win"), ROUNDS * per, 2)
-    white = white[:, :, :width]
-
-    total = windows * hosts
-    count = ROUNDS * per
-    white = white.reshape(total, GROUPS, 16, width).transpose(1, 0, 2, 3).reshape(GROUPS, total * 16, width)
-    mine = mine.reshape(total, GROUPS, 2, 8, count)
-    turned = jnp.stack([mine[:, :, 1], -mine[:, :, 0]], axis=2)
-    rows = jnp.stack([mine, turned]).transpose(2, 5, 0, 1, 3, 4)
-    eye = jnp.eye(8, dtype=jnp.bfloat16)
-    spread = (rows[:, :, :, None] * eye[:, None, None, :]).reshape(GROUPS, count * 16, total * 16)
-    cross = jnp.einsum("gmk,gkc->gmc", spread, white, preferred_element_type=jnp.float32).astype(jnp.bfloat16)
-    cross = cross.reshape(GROUPS, count, 16, width).transpose(1, 0, 2, 3).reshape(count, 2 * BINS, width)
-    lags = jnp.asarray(lag_matrix(1 / math.sqrt(total * BINS))).astype(jnp.bfloat16)
-    out = jnp.einsum("kf,sfc->skc", lags, cross, preferred_element_type=jnp.float32)
-    return out.astype(jnp.bfloat16).reshape(ROUNDS, per, LAGS, width)
+    rows = white[:, :, width:].reshape(windows, GROUPS, 16, -1)
+    rows = jnp.pad(rows.transpose(3, 1, 0, 2), ((0, 0), (0, 0), (0, 64 // 16 - windows), (0, 0)))
+    rows = rows.reshape(hosts, SLOTS, GROUPS // 2, 128).transpose(0, 2, 1, 3)
+    white = lax.all_gather(white[:, :, :width].reshape(windows, GROUPS, 16, width), "win", axis=0)
+    rows = lax.all_gather(rows, "win", axis=0)
+    rows = lax.dynamic_index_in_dim(rows, lax.axis_index("win"), 1, keepdims=False)
+    out = correlations(white, rows, windows * hosts, ROUNDS * per)
+    return out.reshape(ROUNDS, per, LAGS, width)
 
 
 def solution(mesh):

time: 177 us -> 154 us (0.87)
  local copies, waits for them, and re-layouts: 61.1 us -> 21.4 us
  waiting for transfers between devices: 56.1 us -> 73.7 us
  Pallas kernels: 0 us -> 11.4 us
  other arithmetic: 18.2 us -> 9.93 us
  matrix products: 13.6 us -> 9.68 us
    all_gather x1 -> x2, waiting for transfers between devices: 37 us -> 54.4 us  [the longest x1 32.7 us: body(): lax.all_gather(white[:, :, :width].reshape(windows, GROUPS, 16, width), '...]
    slice x3, local copies, waits for them, and re-layouts: 17.5 us -> 2.13 us  [the longest x2 1.21 us: body(): white[:, :, :width].reshape(windows, GROUPS, 16, width)]
    mul x4 -> x0, local copies, waits for them, and re-layouts: 14.3 us -> none  [body(): rows[:, :, :, None] * eye[:, None, None, :]]
    pallas_call x0 -> x1, Pallas kernels: none -> 11.4 us  [correlations(): pl.pallas_call(correlate, grid=(used,), out_shape=jax.ShapeDtypeStruct((u...]
    another operation x2 -> x0, local copies, waits for them, and re-layouts: 8.69 us -> none  [body(): rows = jnp.stack([mine, turned]).transpose(2, 5, 0, 1, 3, 4)]
    mul x1 -> x0, other arithmetic: 6.87 us -> none  [body(): rows[:, :, :, None] * eye[:, None, None, :]]
    dot_general x2 -> x0, matrix products: 3.89 us -> none  [the longest x1 2.86 us: body(): jnp.einsum('gmk,gkc->gmc', spread, white, preferred_element_type=jnp.floa...]
    transpose x2 -> x1, local copies, waits for them, and re-layouts: 4.25 us -> 0.76 us  [body(): rows = rows.reshape(hosts, SLOTS, GROUPS // 2, 128).transpose(0, 2, 1, 3)]
  transfers between devices with their start and end apart: 2 -> 3, of which waited for: 2 -> 3; matrix products, arithmetic and copies ran while one was open for 5% -> 6% of each run, Pallas kernels for 0% -> 0%
where the time goes in v2:
time: 154 us; the launch traced here: 153 us
  waiting for transfers between devices  73.7 us (48%)
  local copies, waits for them, and re-layouts  21.4 us (14%)
  between operations  17.8 us (12%)
  Pallas kernels  11.4 us (7%)
  other arithmetic  9.93 us (6%)
  matrix products  9.68 us (6%)
  starting transfers between devices  9.44 us (6%)
    all_gather x1, waiting for transfers between devices, body(): lax.all_gather(white[:, :, :width].reshape(windows, GROUPS, 16, width), '...  32.7 us
    all_gather x1, waiting for transfers between devices, body(): rows = lax.all_gather(rows, 'win', axis=0)  21.7 us
    all_to_all x1, waiting for transfers between devices, body(): got = lax.all_to_all(sent, 'chan', split_axis=0, concat_axis=0, tiled=True)  19.2 us
    pallas_call x1, Pallas kernels, correlations(): pl.pallas_call(correlate, grid=(used,), out_shape=jax.ShapeDtypeStruct((u...  11.4 us
    all_to_all x1, starting transfers between devices, body(): got = lax.all_to_all(sent, 'chan', split_axis=0, concat_axis=0, tiled=True)  9.35 us
    unnamed x17, local copies, waits for them, and re-layouts  7.24 us
    dot_general x1, matrix products, body(): jnp.einsum('wrj,wjc->wrc', pair, record, preferred_element_type=jnp.float32)  7.05 us
    reshape x1, local copies, waits for them, and re-layouts, body(): rows = rows.reshape(hosts, SLOTS, GROUPS // 2, 128).transpose(0, 2, 1, 3)  3.54 us
  transfers between devices with their start and end apart: 3, of which 3 were waited for; matrix products, arithmetic and copies ran while one was open for 6% of the time, Pallas kernels for 0%

profile of v2, /device:TPU:1, one launch (start us, length us, event | category | flops | bytes accessed | tf_op | source)
XLA Modules:
  0.0 153.3 jit_solution(9626054967693753696)
XLA Ops:
  6.5 0.7 fusion.33
  7.3 0.8 fusion.23
  8.0 0.8 select_convert_fusion
  8.8 7.1 %fusion.24 = f32[3,64,8192]{2,1,0:T(8,128)S(1)} fusion(bf16[3,248,8192]{2,1,0:T(8,128)(2,1)} %param.6, bf16[3,32,248]{2,1,0:T(8,128)(2,1)S(1)} %fusion.23, bf16[3,32,248]{2,1,0:T(8,128)(2,1)S(1)} %select_convert_fusion), kind=kOutput, calls=%fused_computation.57 | convolution fusion | flops 780331008 | bytes 18576384 | tf_op jit(solution)/shard_map/wrj,wjc->wrc/dot_general | solution.py:132
  15.9 0.3 fusion
  16.2 0.4 copy-done.6
  16.6 0.1 reshape.597
  16.6 0.1 reshape.598
  16.7 0.1 eq.18
  16.8 0.6 fusion.4
  17.5 0.2 copy-done.2
  17.7 1.6 %copy.36 = bf16[3,4,32,8,256]{4,3,1,0,2:T(8,128)(2,1)S(1)} copy(bf16[3,4,32,8,256]{4,3,2,1,0:T(8,128)(2,1)} %bitcast.105) | data formatting | bytes 3145728 | tf_op jit(solution)/shard_map/reshape | solution.py:141
  19.3 0.1 broadcast_in_dim.25
  19.4 1.8 %pad_maximum_fusion = bf16[32,3,32,320]{3,2,1,0:T(8,128)(2,1)} fusion(bf16[32,3,32,64]{3,2,1,0:T(8,128)(2,1)S(1)} %broadcast_in_dim.25, bf16[32,3,32,256]{3,2,1,0:T(8,128)(2,1)S(1)} %bitcast.104), kind=kLoop, calls=%fused_computation.2 | loop fusion | flops 3932160 | bytes 3932160 | tf_op jit(solution)/shard_map/concatenate | solution.py:143
  21.2 9.4 %all-to-all-start = ((bf16[32,3,32,320]{3,2,1,0:T(8,128)(2,1)}), bf16[32,3,32,320]{3,2,1,0:T(8,128)(2,1)S(1)}, u32[]{:S(2)}, u32[]{:S(2)}) async-start(bf16[32,3,32,320]{3,2,1,0:T(8,128)(2,1)} %pad_maximum_fusion), calls=%async_computation | async-start | bytes 4718592 | tf_op jit(solution)/shard_map/all_to_all | solution.py:144
  30.6 0.7 fusion.36
  35.5 0.1 fusion.29
  35.6 0.1 cosine_reduce_fusion.2
  35.7 0.1 sin.51
  35.8 0.1 cos.49
  35.9 0.1 sin.59
  36.0 0.1 cos.57
  36.1 0.1 sin.55
  36.2 0.1 cos.53
  36.3 3.4 %fusion.16 = (bf16[32,1,8,1024]{3,2,1,0:T(8,128)(2,1)S(1)}, bf16[32,1,8,1024]{3,2,1,0:T(8,128)(2,1)S(1)}, bf16[32,1,8,1024]{3,2,1,0:T(8,128)(2,1)S(1)}, bf16[32,...) fusion(f32[1,1,256,1024]{3,2,1,0:T(8,128)S(1)} %copy-done.5, ...), kind=kLoop, calls=%fused_computation.30 | loop fusion | flops 12582912 | bytes 9443352 | tf_op jit(solution)/shard_map/convert.4
  39.7 0.1 pad_maximum_fusion.3
  39.8 1.5 pad_maximum_fusion.1
  41.3 19.2 %all-to-all-done = bf16[32,3,32,320]{3,2,1,0:T(8,128)(2,1)S(1)} async-done(((bf16[32,3,32,320]{3,2,1,0:T(8,128)(2,1)}), bf16[32,3,32,320]{3,2,1,0:T(8,128)(2,1)S(1)}, u32[]{:S(2)}, u32[]{:S(2)}) %all-to-all-start) | async-done | bytes 1966112 | tf_op jit(solution)/shard_map/all_to_all | solution.py:144
  60.5 0.3 fusion.35
  60.8 0.7 multiply_reduce_fusion
  61.5 0.5 copy-done.4
  62.0 0.7 multiply_reduce_fusion.1
  62.7 0.7 multiply_reduce_fusion.2
  63.4 0.1 fusion.22
  63.5 0.1 fusion.21
  63.6 0.1 fusion.20
  63.8 0.9 copy.30
  64.7 4.2 %copy.33 = bf16[64,32,3,16]{3,2,1,0:T(4,128)(2,1)S(1)} copy(bf16[64,32,3,16]{0,3,1,2:T(8,128)(2,1)} %bitcast.113) | data formatting | bytes 393216
  68.9 3.2 %pad.9.clone = bf16[64,32,4,16]{3,2,1,0:T(4,128)(2,1)} pad(bf16[64,32,3,16]{3,2,1,0:T(4,128)(2,1)S(1)} %copy.33, bf16[]{:T(256)} %constant.51.clone.1), padding=0_0x0_0x0_1x0_0 | pad | bytes 458754 | tf_op jit(solution)/shard_map/jit(_pad)/pad | solution.py:164
  72.1 3.5 %reshape.600 = bf16[4,16,16,128]{3,2,1,0:T(8,128)(2,1)S(1)} reshape(bf16[64,32,4,16]{3,2,1,0:T(4,128)(2,1)} %pad.9.clone) | data formatting | bytes 524288 | tf_op jit(solution)/shard_map/reshape | solution.py:165
  75.6 0.8 copy.32
  76.4 0.1 pad_maximum_fusion.4
  76.6 1.2 copy.29
  77.8 21.7 %all-gather.6.cloned.1.call-done = bf16[16,16,16,128]{3,2,1,0:T(8,128)(2,1)} async-done(((bf16[4,16,16,128]{3,2,1,0:T(8,128)(2,1)}), bf16[16,16,16,128]{3,2,1,0:T(8,128)(2,1)}) %all-gather.6.cloned.1.call-update) | async-done | bytes 1048592 | tf_op jit(solution)/shard_map/all_gather | solution.py:167
  99.5 1.0 dynamic-slice_bitcast_fusion.rows_ref
  100.5 32.7 %all-gather.4.cloned.1.call-done.white_ref = bf16[4,3,32,16,256]{4,3,2,1,0:T(8,128)(2,1)} async-done(((bf16[1,3,32,16,256]{4,3,2,1,0:T(8,128)(2,1)}), bf16[4,3,32,16,256]{4,3,2,1,0:T(8,128)(2,1)}) %all-gather.4.cloned.1.call-update) | async-done | bytes 3145744 | tf_op jit(solution)/shard_map/all_gather | solution.py:166
  133.2 1.9 %copy-done = bf16[4,3,32,16,256]{4,3,2,1,0:T(8,128)(2,1)S(1)} copy-done((bf16[4,3,32,16,256]{4,3,2,1,0:T(8,128)(2,1)S(1)}, bf16[4,3,32,16,256]{4,3,2,1,0:T(8,128)(2,1)}, u32[]{:S(2)}) %copy-start) | copy-done | bytes 3145752
  135.1 11.4 %shard_map.64 = bf16[12,256,256]{2,1,0:T(8,128)(2,1)} custom-call(bf16[4,3,32,16,256]{4,3,2,1,0:T(8,128)(2,1)S(1)} %copy-done, bf16[4,16,16,128]{3,2,1,0:T(8,128)(2,1)S(1)} %dynamic-slice_bitcast_fusion.rows_ref, bf16[512,512]{1,0:T(8,128)(2,1)S(1)} %copy-done.1), custom_call_target="tpu_custom_call" | custom-call | tf_op jit(solution)/shard_map/pallas_call | solution.py:105
  (26 shorter events, 0.3 us)
Async XLA Ops:
  15.9 0.7 copy-start.6
  16.6 1.1 copy-start.2
  21.2 9.4 %copy-start.7 = (s32[3]{0:T(128)S(1)}, s32[3]{0:T(128)}, u32[]{:S(2)}) copy-start(s32[3]{0:T(128)} %param.7) | copy-start | bytes 40
  21.2 15.1 %copy-start.5 = (f32[1,1,256,1024]{3,2,1,0:T(8,128)S(1)}, f32[1,1,256,1024]{3,2,1,0:T(8,128)}, u32[]{:S(2)}) copy-start(f32[1,1,256,1024]{3,2,1,0:T(8,128)} %constant.69) | copy-start | bytes 3145732
  21.2 39.3 %all-to-all-start = ((bf16[32,3,32,320]{3,2,1,0:T(8,128)(2,1)}), bf16[32,3,32,320]{3,2,1,0:T(8,128)(2,1)S(1)}, u32[]{:S(2)}, u32[]{:S(2)}) async-start(bf16[32,3,32,320]{3,2,1,0:T(8,128)(2,1)} %pad_maximum_fusion), calls=%async_computation | async-start | bytes 4718592 | tf_op jit(solution)/shard_map/all_to_all | solution.py:144
  30.6 69.0 %all-gather.6.cloned.1.call-start = ((), (), s32[]{:S(2)}) async-start(), calls=%async_computation.2 | async-start | bytes 1310720 | tf_op jit(solution)/shard_map/all_gather | solution.py:167
  60.8 1.2 copy-start.4
  60.8 1.9 %copy-start.3 = (bf16[32,2,8,1024]{3,2,1,0:T(8,128)(2,1)S(1)}, bf16[32,2,8,1024]{3,2,1,0:T(8,128)(2,1)}, u32[]{:S(2)}) copy-start(bf16[32,2,8,1024]{3,2,1,0:T(8,128)(2,1)} %get-tuple-element.33) | copy-start | bytes 3145732
  76.4 56.8 %all-gather.4.cloned.1.call-start = ((), (), s32[]{:S(2)}) async-start(), calls=%async_computation.1 | async-start | bytes 3932160 | tf_op jit(solution)/shard_map/all_gather | solution.py:166
  76.5 56.6 %copy-start.1 = (bf16[512,512]{1,0:T(8,128)(2,1)S(1)}, bf16[512,512]{1,0:T(8,128)(2,1)}, u32[]{:S(2)}) copy-start(bf16[512,512]{1,0:T(8,128)(2,1)} %constant.74.lag_ref) | copy-start | bytes 1572868
  133.2 1.9 %copy-start = (bf16[4,3,32,16,256]{4,3,2,1,0:T(8,128)(2,1)S(1)}, bf16[4,3,32,16,256]{4,3,2,1,0:T(8,128)(2,1)}, u32[]{:S(2)}) copy-start(bf16[4,3,32,16,256]{4,3,2,1,0:T(8,128)(2,1)} %all-gather.4.cloned.1.call-done.white_ref) | copy-start | bytes 9437188
Sparse Core Ops, SparseCore 0:
  76.5 22.9 all-gather.5
  101.2 31.9 all-gather.3

commit v3 on v2

--- a/solution.py
+++ b/solution.py
@@ -17,6 +17,7 @@
 RANK = 32
 GROUPS = BINS // 8
 SLOTS = 16
+MESH = pl.DeviceIdType.MESH
 
 
 def sample_basis(count):
@@ -38,9 +39,10 @@
         freqs = np.arange(BINS) + F0 + step
         wave = np.exp(-2j * math.pi / SAMPLES * np.outer(freqs, at)) @ basis
         turn = np.exp(-2j * math.pi / SAMPLES * np.outer(freqs, count * np.arange(blocks) + middle))
-        terms.append(weight * (turn[:, :, None] * wave[:, None, :]).reshape(BINS, blocks * RANK))
+        table = weight * (turn[:, :, None] * wave[:, None, :]).reshape(BINS, blocks, 2, RANK // 2)
+        terms.append(table.transpose(0, 2, 1, 3).reshape(BINS, blocks * RANK))
     own, above, below = terms
-    return np.stack([np.stack([t.real, t.imag]) for t in (own, above + below, above - below)]).astype(np.float32)
+    return np.stack([p for t in (own, above + below, above - below) for p in (t.real, t.imag)]).astype(np.float32)
 
 
 def lag_matrix(scale):
@@ -54,6 +56,289 @@
 def split_pair(array):
     high = array.astype(jnp.bfloat16)
     return high, (array - high.astype(jnp.float32)).astype(jnp.bfloat16)
+
+
+def exchange(
+    record, tables, basis, turns, picks, white_out, rows_out,
+    held, parts, message, arrived, coded, full, spectra, columns, whites, rows,
+    load_sem, table_sem, send_sem, recv_sem, pass_sem, take_sem, rows_send, rows_recv, own_sem,
+):
+    windows, chunks = held.shape[:2]
+    blocks = message.shape[1]
+    count = picks.shape[1]
+    me, win = lax.axis_index("chan"), lax.axis_index("win")
+
+    def load(w, k):
+        at = (me // 4) ^ k
+        source = record.at[w, :, pl.ds(pl.multiple_of(at * 1024, 1024), 1024)]
+        return pltpu.make_async_copy(source, held.at[w, k], load_sem.at[w, k])
+
+    def start_load(i, _):
+        load(i // chunks, i % chunks).start()
+        return 0
+
+    lax.fori_loop(0, windows * chunks, start_load, 0)
+    table_copy = pltpu.make_async_copy(tables, parts, table_sem)
+    table_copy.start()
+
+    barrier = pltpu.get_barrier_semaphore()
+
+    def greet(k, _):
+        pl.semaphore_signal(barrier, inc=1, device_id=(win, me ^ k), device_id_type=MESH)
+        return 0
+
+    lax.fori_loop(1, blocks, greet, 0)
+    for k in (1, 2, 3):
+        pl.semaphore_signal(barrier, inc=1, device_id=(win ^ k, me), device_id_type=MESH)
+
+    lane = lax.broadcasted_iota(jnp.int32, (16, 128), 1)
+    columns[:, 48:, :] = jnp.zeros((GROUPS, 16, 128), jnp.float32)
+
+    def project(w):
+        def chunk(k, _):
+            load(w, k).wait()
+            at = (me // 4) ^ k
+            found = jnp.dot(basis[w], held[w, k], preferred_element_type=jnp.float32)
+            found = (found[:RANK] + found[RANK:]).astype(jnp.bfloat16)
+            for i in range(4):
+                part = found[:, 256 * i : 256 * (i + 1)]
+                message[w, at * 4 + i, :, 0:256] = part[:16]
+                message[w, at * 4 + i, :, 256:512] = part[16:]
+            for i in range(8):
+                coded[at * 8 + i] = found[:, 128 * i : 128 * (i + 1)]
+            return 0
+
+        lax.fori_loop(0, chunks, chunk, 0)
+
+        def pick(i, total):
+            tile = coded[picks[0, i]].astype(jnp.float32)
+            wide = lax.broadcasted_iota(jnp.int32, (RANK, 128), 1)
+            value = jnp.sum(jnp.where(wide == picks[1, i], tile, 0.0), axis=1, keepdims=True)
+            slot = i // 12 * SLOTS + i % 12
+            total = jnp.where(lane == slot, value[:16], total)
+            return jnp.where(lane == slot + 64, value[16:], total)
+
+        chosen = lax.fori_loop(0, count, pick, jnp.zeros((16, 128), jnp.float32)).astype(jnp.bfloat16)
+
+        def fill(c, _):
+            message[w, c, :, 512:640] = chosen
+            return 0
+
+        lax.fori_loop(0, blocks, fill, 0)
+        arrived[w, me] = message[w, me]
+
+    def send(w, k):
+        return pltpu.make_async_remote_copy(
+            message.at[w, me ^ k], arrived.at[w, me], send_sem.at[w, k], recv_sem.at[w, me],
+            device_id=(win, me ^ k), device_id_type=MESH,
+        )
+
+    def receive(w, k):
+        return pltpu.make_async_remote_copy(
+            message.at[w, me ^ k], arrived.at[w, me ^ k], send_sem.at[w, k], recv_sem.at[w, me ^ k],
+            device_id=(win, me ^ k), device_id_type=MESH,
+        )
+
+    def start_sends(w):
+        def one(k, _):
+            send(w, k).start()
+            return 0
+
+        lax.fori_loop(1, blocks, one, 0)
+
+    project(0)
+    pl.semaphore_wait(barrier, blocks - 1 + 3)
+    start_sends(0)
+
+    def later(w, _):
+        project(w)
+        start_sends(w)
+        return 0
+
+    lax.fori_loop(1, windows, later, 0)
+
+    table_copy.wait()
+
+    def tabulate(i, _):
+        w, g = i // GROUPS, i % GROUPS
+        own_re, own_im, sum_re, sum_im, dif_re, dif_im = [parts[t, pl.ds(pl.multiple_of(g * 8, 8), 8)] for t in range(6)]
+        turn = turns[w, pl.ds(pl.multiple_of(g * 8, 8), 8)]
+        c, s = turn[:, 2:3], turn[:, 3:4]
+        re = own_re + c * sum_re - s * dif_im
+        im = own_im + c * sum_im + s * dif_re
+        c, s = turn[:, 0:1], turn[:, 1:2]
+        both = jnp.concatenate([c * re - s * im, c * im + s * re], axis=0)
+        high = both.astype(jnp.bfloat16)
+        full[w, 0, g] = high
+        full[w, 1, g] = (both - high.astype(jnp.float32)).astype(jnp.bfloat16)
+        return 0
+
+    lax.fori_loop(0, windows * GROUPS, tabulate, 0)
+
+    def hand(w, k):
+        return pltpu.make_async_remote_copy(
+            whites.at[w], white_out.at[win, w], pass_sem.at[k - 1, w], take_sem.at[k - 1, w],
+            device_id=(win ^ k, me), device_id_type=MESH,
+        )
+
+    def taken(w, k):
+        return pltpu.make_async_remote_copy(
+            whites.at[w], white_out.at[win ^ k, w], pass_sem.at[k - 1, w], take_sem.at[k - 1, w],
+            device_id=(win ^ k, me), device_id_type=MESH,
+        )
+
+    def relay(w, owner):
+        return pltpu.make_async_remote_copy(
+            white_out.at[owner, w], white_out.at[owner, w], pass_sem.at[2, w], take_sem.at[2, w],
+            device_id=(win ^ 1, me), device_id_type=MESH,
+        )
+
+    def keep(w):
+        return pltpu.make_async_copy(whites.at[w], white_out.at[win, w], own_sem.at[w])
+
+    def whiten(w, _):
+        def wait_one(k, _):
+            receive(w, k).wait_recv()
+            return 0
+
+        lax.fori_loop(1, blocks, wait_one, 0)
+        first = arrived[w, :, :, 0:256].reshape(blocks * 16, 256)
+        second = arrived[w, :, :, 256:512].reshape(blocks * 16, 256)
+        extra = arrived[w, :, :, 512:640].reshape(blocks * 16, 128)
+        cut = blocks * 16
+
+        def tile(m, power):
+            found = jnp.zeros((128, 256), jnp.float32)
+            low = jnp.zeros((128, 128), jnp.float32)
+            top = jnp.zeros((128, 128), jnp.float32)
+            for half in range(2):
+                table = full[w, half, pl.ds(m * 8, 8)].reshape(128, 2 * cut)
+                left, right = table[:, :cut], table[:, cut:]
+                found += jnp.dot(left, first, preferred_element_type=jnp.float32)
+                found += jnp.dot(right, second, preferred_element_type=jnp.float32)
+                low += jnp.dot(left, extra, preferred_element_type=jnp.float32)
+                top += jnp.dot(right, extra, preferred_element_type=jnp.float32)
+            rows_at = pl.ds(pl.multiple_of(m * 128, 128), 128)
+            spectra[rows_at, 0:256] = found
+            mine = low + pltpu.roll(top, 64, 1)
+            spectra[rows_at, 256:384] = mine
+            return power[0] + jnp.sum(found * found, axis=0, keepdims=True), power[1] + jnp.sum(mine * mine, axis=0, keepdims=True)
+
+        zero = jnp.zeros((1, 256), jnp.float32), jnp.zeros((1, 128), jnp.float32)
+        power = lax.fori_loop(0, 4, tile, zero)
+        scale, scale_picked = [lax.rsqrt(p * (1 / (2 * BINS)) + 1e-06) for p in power]
+
+        def norm(m, _):
+            rows_at = pl.ds(pl.multiple_of(m * 128, 128), 128)
+            white = (spectra[rows_at, 0:256] * scale).astype(jnp.bfloat16)
+            whites[w, pl.ds(m * 8, 8)] = white.reshape(8, 16, 256)
+            white = (spectra[rows_at, 256:384] * scale_picked).astype(jnp.bfloat16).astype(jnp.float32)
+            columns[pl.ds(m * 8, 8), pl.ds(pl.multiple_of(w * 16, 16), 16)] = white.reshape(8, 16, 128)
+            return 0
+
+        lax.fori_loop(0, 4, norm, 0)
+        hand(w, 2).start()
+        hand(w, 1).start()
+        keep(w).start()
+        return 0
+
+    lax.fori_loop(0, windows, whiten, 0)
+
+    def turn_over(at, _):
+        block = columns[pl.ds(at * 2, 2)].reshape(128, 128).T
+        rows[:, at] = block[:64].reshape(4, SLOTS, 128).astype(jnp.bfloat16)
+        return 0
+
+    lax.fori_loop(0, GROUPS // 2, turn_over, 0)
+
+    def deal(k):
+        return pltpu.make_async_remote_copy(
+            rows.at[win ^ k], rows_out.at[win], rows_send.at[k], rows_recv.at[k],
+            device_id=(win ^ k, me), device_id_type=MESH,
+        )
+
+    def dealt(k):
+        return pltpu.make_async_remote_copy(
+            rows.at[win ^ k], rows_out.at[win ^ k], rows_send.at[k], rows_recv.at[k],
+            device_id=(win ^ k, me), device_id_type=MESH,
+        )
+
+    for k in (3, 2, 1):
+        deal(k).start()
+    own_rows = pltpu.make_async_copy(rows.at[win], rows_out.at[win], rows_send.at[0])
+    own_rows.start()
+
+    def forward(w, _):
+        taken(w, 2).wait_recv()
+        relay(w, win ^ 2).start()
+        return 0
+
+    lax.fori_loop(0, windows, forward, 0)
+
+    def finish(w, _):
+        keep(w).wait()
+        hand(w, 1).wait_send()
+        hand(w, 2).wait_send()
+        taken(w, 1).wait_recv()
+        relay(w, win ^ 2).wait_send()
+        relay(w, win ^ 3).wait_recv()
+
+        def sent(k, _):
+            send(w, k).wait_send()
+            return 0
+
+        lax.fori_loop(1, blocks, sent, 0)
+        return 0
+
+    lax.fori_loop(0, windows, finish, 0)
+    own_rows.wait()
+    for k in (1, 2, 3):
+        deal(k).wait_send()
+        dealt(k).wait_recv()
+
+
+def exchanged(record, tables, basis, turns, picks, blocks, hosts):
+    windows, count, channels = record.shape
+    width = channels // blocks
+    dma = pltpu.SemaphoreType.DMA
+    anywhere = pl.BlockSpec(memory_space=pl.ANY)
+    return pl.pallas_call(
+        exchange,
+        out_shape=(
+            jax.ShapeDtypeStruct((hosts, windows, GROUPS, 16, width), jnp.bfloat16),
+            jax.ShapeDtypeStruct((hosts, GROUPS // 2, SLOTS, 128), jnp.bfloat16),
+        ),
+        in_specs=[
+            anywhere,
+            anywhere,
+            pl.BlockSpec(memory_space=pltpu.VMEM),
+            pl.BlockSpec(memory_space=pltpu.VMEM),
+            pl.BlockSpec(memory_space=pltpu.SMEM),
+        ],
+        out_specs=(anywhere, anywhere),
+        scratch_shapes=[
+            pltpu.VMEM((windows, 8, count, channels // 8), jnp.bfloat16),
+            pltpu.VMEM(tables.shape, jnp.float32),
+            pltpu.VMEM((windows, blocks, 16, 640), jnp.bfloat16),
+            pltpu.VMEM((windows, blocks, 16, 640), jnp.bfloat16),
+            pltpu.VMEM((channels // 128, RANK, 128), jnp.bfloat16),
+            pltpu.VMEM((windows, 2, GROUPS, 16, blocks * RANK), jnp.bfloat16),
+            pltpu.VMEM((2 * BINS, 384), jnp.float32),
+            pltpu.VMEM((GROUPS, 64, 128), jnp.float32),
+            pltpu.VMEM((windows, GROUPS, 16, width), jnp.bfloat16),
+            pltpu.VMEM((hosts, GROUPS // 2, SLOTS, 128), jnp.bfloat16),
+            dma((windows, 8)),
+            dma,
+            dma((windows, blocks)),
+            dma((windows, blocks)),
+            dma((3, windows)),
+            dma((3, windows)),
+            dma((4,)),
+            dma((4,)),
+            dma((windows,)),
+        ],
+        compiler_params=pltpu.CompilerParams(collective_id=0, has_side_effects=True, vmem_limit_bytes=48 << 20),
+    )(record, tables, basis, turns, picks)
 
 
 def correlate(white_ref, rows_ref, lag_ref, out_ref, cross):
@@ -125,47 +410,23 @@
 
     at = first + jnp.arange(count, dtype=jnp.int32)[None, :] - offsets[:, None]
     inside = (at >= 0) & (at < SAMPLES)
-    basis = jnp.asarray(sample_basis(count).T.astype(np.float32))
-    masked = jnp.where(inside[:, None, :], basis[None], 0.0)
-    high, low = split_pair(masked)
-    pair = jnp.concatenate([high, low], axis=1)
-    coef = jnp.einsum("wrj,wjc->wrc", pair, record, preferred_element_type=jnp.float32)
-    coef = (coef[:, :RANK] + coef[:, RANK:]).astype(jnp.bfloat16)
+    basis = sample_basis(count).T.astype(np.float32)
+    high = basis.astype(jnp.bfloat16)
+    low = (basis - high.astype(np.float32)).astype(jnp.bfloat16)
+    basis = jnp.where(inside[:, None, :], jnp.asarray(np.concatenate([high, low]))[None], 0.0)
 
     per = sources.shape[1] // hosts
-    wanted = sources.reshape(ROUNDS, hosts, per).transpose(1, 0, 2).reshape(hosts, ROUNDS * per)
-    wanted = jnp.pad(wanted, ((0, 0), (0, SLOTS - ROUNDS * per)), constant_values=-1).reshape(-1)
-    onehot = (jnp.arange(channels, dtype=jnp.int32)[:, None] == wanted[None, :]).astype(jnp.bfloat16)
-    picked = jnp.einsum("wrc,cs->wrs", coef, onehot, preferred_element_type=jnp.float32).astype(jnp.bfloat16)
-
-    cut = coef.reshape(windows, RANK, blocks, width).transpose(2, 0, 1, 3)
-    extra = jnp.broadcast_to(picked[None], (blocks,) + picked.shape)
-    sent = jnp.concatenate([cut, extra], axis=3)
-    got = lax.all_to_all(sent, "chan", split_axis=0, concat_axis=0, tiled=True)
-    got = got.transpose(1, 0, 2, 3).reshape(windows, blocks * RANK, -1)
-
-    tables = jnp.asarray(spectrum_tables(count, blocks))
+    wanted = sources.reshape(ROUNDS, hosts, per).transpose(1, 0, 2).reshape(-1)
+    picks = jnp.stack([wanted // 128, wanted % 128])
+
     freqs = jnp.arange(BINS, dtype=jnp.int32) + F0
     turn = 2 * math.pi / SAMPLES * (freqs[None, :] * offsets[:, None] % SAMPLES).astype(jnp.float32)
-    step = 2 * math.pi / SAMPLES * offsets.astype(jnp.float32)
-    white = []
-    for w in range(windows):
-        c, s = jnp.cos(step[w]), jnp.sin(step[w])
-        re = tables[0, 0] + c * tables[1, 0] - s * tables[2, 1]
-        im = tables[0, 1] + c * tables[1, 1] + s * tables[2, 0]
-        c, s = jnp.cos(turn[w])[:, None], jnp.sin(turn[w])[:, None]
-        full = jnp.stack([(c * re - s * im).reshape(GROUPS, 8, -1), (c * im + s * re).reshape(GROUPS, 8, -1)], axis=1)
-        full = full.reshape(2 * BINS, -1).astype(jnp.bfloat16)
-        spectra = jnp.dot(full, got[w], preferred_element_type=jnp.float32)
-        power = jnp.mean(spectra * spectra, axis=0, keepdims=True)
-        white.append((spectra * lax.rsqrt(power + 1e-06)).astype(jnp.bfloat16))
-    white = jnp.stack(white)
-    rows = white[:, :, width:].reshape(windows, GROUPS, 16, -1)
-    rows = jnp.pad(rows.transpose(3, 1, 0, 2), ((0, 0), (0, 0), (0, 64 // 16 - windows), (0, 0)))
-    rows = rows.reshape(hosts, SLOTS, GROUPS // 2, 128).transpose(0, 2, 1, 3)
-    white = lax.all_gather(white[:, :, :width].reshape(windows, GROUPS, 16, width), "win", axis=0)
-    rows = lax.all_gather(rows, "win", axis=0)
-    rows = lax.dynamic_index_in_dim(rows, lax.axis_index("win"), 1, keepdims=False)
+    step = jnp.broadcast_to(2 * math.pi / SAMPLES * offsets.astype(jnp.float32)[:, None], turn.shape)
+    turns = jnp.stack([jnp.cos(turn), jnp.sin(turn), jnp.cos(step), jnp.sin(step)], axis=2)
+    turns = jnp.pad(turns, ((0, 0), (0, 0), (0, 124)))
+
+    tables = jnp.asarray(spectrum_tables(count, blocks))
+    white, rows = exchanged(record, tables, basis, turns, picks, blocks, hosts)
     out = correlations(white, rows, windows * hosts, ROUNDS * per)
     return out.reshape(ROUNDS, per, LAGS, width)
 

time: 154 us -> 75.8 us (0.49)
  waiting for transfers between devices: 73.7 us -> 0 us
  Pallas kernels: 11.4 us -> 71.2 us
  local copies, waits for them, and re-layouts: 21.4 us -> 1.22 us
  between operations: 17.8 us -> 0.08 us
  matrix products: 9.68 us -> 0 us
  starting transfers between devices: 9.44 us -> 0 us
  other arithmetic: 9.93 us -> 3.09 us
    pallas_call x0 -> x1, Pallas kernels: none -> 59.8 us  [exchanged(): pl.pallas_call(exchange, out_shape=(jax.ShapeDtypeStruct((hosts, windows,...]
    all_gather x2 -> x0, waiting for transfers between devices: 54.4 us -> none  [the longest x1 32.7 us: body(): lax.all_gather(white[:, :, :width].reshape(windows, GROUPS, 16, width), '...]
    all_to_all x1 -> x0, waiting for transfers between devices: 19.2 us -> none  [body(): got = lax.all_to_all(sent, 'chan', split_axis=0, concat_axis=0, tiled=True)]
    dot_general x5 -> x0, matrix products: 9.68 us -> none  [the longest x1 7.05 us: body(): jnp.einsum('wrj,wjc->wrc', pair, record, preferred_element_type=jnp.float32)]
    all_to_all x1 -> x0, starting transfers between devices: 9.35 us -> none  [body(): got = lax.all_to_all(sent, 'chan', split_axis=0, concat_axis=0, tiled=True)]
    unnamed x17 -> x2, local copies, waits for them, and re-layouts: 7.24 us -> 0.01 us
    another operation x7 -> x2, other arithmetic: 5.46 us -> 0.03 us  [the longest x1 0.02 us: body(): jnp.stack([jnp.cos(turn), jnp.sin(turn), jnp.cos(step), jnp.sin(step)], a...]
    reshape x4 -> x2, local copies, waits for them, and re-layouts: 5.32 us -> 0.85 us  [body(): wanted = sources.reshape(ROUNDS, hosts, per).transpose(1, 0, 2).reshape(-1)]
  transfers between devices with their start and end apart: 3 -> 0, of which waited for: 3 -> 0; matrix products, arithmetic and copies ran while one was open for 6% -> 0% of each run, Pallas kernels for 0% -> 0%
where the time goes in v3:
time: 75.8 us; the launch traced here: 75.6 us
  Pallas kernels  71.2 us (94%)
  other arithmetic  3.09 us (4%)
  local copies, waits for them, and re-layouts  1.22 us (2%)
    pallas_call x1, Pallas kernels, exchanged(): pl.pallas_call(exchange, out_shape=(jax.ShapeDtypeStruct((hosts, windows,...  59.8 us
    pallas_call x1, Pallas kernels, correlations(): pl.pallas_call(correlate, grid=(used,), out_shape=jax.ShapeDtypeStruct((u...  11.5 us

profile of v3, /device:TPU:1, one launch (start us, length us, event | category | flops | bytes accessed | tf_op | source)
XLA Modules:
  0.0 75.6 jit_solution(16820199467727988533)
XLA Ops:
  0.0 0.7 fusion
  0.7 0.7 fusion.4
  1.4 0.1 stack.16
  1.5 0.1 stack.17
  1.6 0.8 %fusion.6 = (f32[3,256,1]{1,2,0:T(1,128)S(1)}, f32[3,256,1]{1,2,0:T(1,128)S(1)}) fusion(s32[3]{0:T(128)} %param.7, s32[256]{0:T(256)S(1)} %iota_add_fusion), kind=kLoop, calls=%fused_computation.20 | loop fusion | flops 6912 | bytes 7180 | tf_op jit(solution)/shard_map/cos | solution.py:425
  2.4 0.8 %reshape.260 = s32[3,4,4]{2,1,0:T(4,128)S(1)} reshape(s32[3,16]{1,0:T(4,128)} %param.8) | data formatting | bytes 384 | tf_op jit(solution)/shard_map/reshape | solution.py:419
  3.2 0.1 reshape.261
  3.3 0.8 %broadcast_select_fusion.basis = bf16[3,64,248]{2,1,0:T(8,128)(2,1)S(1)} fusion(pred[3,248]{1,0:T(4,128)(4,1)S(1)} %fusion, bf16[64,248]{1,0:T(8,128)(2,1)} %constant.64.clone), kind=kLoop, calls=%fused_computation | loop fusion | flops 47616 | bytes 127720 | tf_op jit(solution)/shard_map/jit(_where)/select_n | solution.py:416
  4.1 0.2 copy.9
  4.4 0.0 copy-start
  4.4 59.8 %shard_map.64 = (bf16[4,3,32,16,256]{4,3,2,1,0:T(8,128)(2,1)S(1)}, bf16[4,16,16,128]{3,2,1,0:T(8,128)(2,1)S(1)}) custom-call(bf16[3,248,8192]{2,1,0:T(8,128)(2,1)} %record.1, f32[6,256,1024]{2,1,0:T(8,128)} %constant.65.clone.tables, bf16[3,64,248]{2,1,0:T(8,128)(2,1)S(1)} %broadcast_select_fusion.basis, f32[3,256,128]{2,1,0:T(8,128)S(1)} %pad.4.turns, ...), custom_call_target="tpu_custom_call" | custom-call | tf_op jit(solution)/shard_map/pallas_call | solution.py:305
  64.1 0.0 copy-done
  64.2 11.5 %shard_map.65 = bf16[12,256,256]{2,1,0:T(8,128)(2,1)} custom-call(bf16[4,3,32,16,256]{4,3,2,1,0:T(8,128)(2,1)S(1)} %get-tuple-element.7.white_ref, bf16[4,16,16,128]{3,2,1,0:T(8,128)(2,1)S(1)} %get-tuple-element.8.rows_ref, bf16[512,512]{1,0:T(8,128)(2,1)S(1)} %copy-done), custom_call_target="tpu_custom_call" | custom-call | tf_op jit(solution)/shard_map/pallas_call | solution.py:390
  (7 shorter events, 0.1 us)
Async XLA Ops:
  4.4 59.8 %copy-start = (bf16[512,512]{1,0:T(8,128)(2,1)S(1)}, bf16[512,512]{1,0:T(8,128)(2,1)}, u32[]{:S(2)}) copy-start(bf16[512,512]{1,0:T(8,128)(2,1)} %constant.75.lag_ref) | copy-start | bytes 1572868

commit v4 on v3

--- a/solution.py
+++ b/solution.py
@@ -55,17 +55,18 @@
 
 def split_pair(array):
     high = array.astype(jnp.bfloat16)
-    return high, (array - high.astype(jnp.float32)).astype(jnp.bfloat16)
+    return high, (array - high.astype(array.dtype)).astype(jnp.bfloat16)
 
 
 def exchange(
-    record, tables, basis, turns, picks, white_out, rows_out,
-    held, parts, message, arrived, coded, full, spectra, columns, whites, rows,
-    load_sem, table_sem, send_sem, recv_sem, pass_sem, take_sem, rows_send, rows_recv, own_sem,
+    record, tables, basis, offsets, sources, white_out, rows_out,
+    held, parts, masked, turns, message, arrived, coded, picked, full, spectra, columns, whites, rows,
+    load_sem, table_sem, send_sem, recv_sem, pass_sem, take_sem, rows_send, rows_recv, own_sem, pick_send, pick_recv,
 ):
     windows, chunks = held.shape[:2]
     blocks = message.shape[1]
-    count = picks.shape[1]
+    samples = held.shape[2]
+    slots = sources.shape[1] // 4
     me, win = lax.axis_index("chan"), lax.axis_index("win")
 
     def load(w, k):
@@ -91,6 +92,21 @@
     for k in (1, 2, 3):
         pl.semaphore_signal(barrier, inc=1, device_id=(win ^ k, me), device_id_type=MESH)
 
+    for w in range(windows):
+        time = lax.broadcasted_iota(jnp.int32, basis.shape, 1) + (me * samples - offsets[w])
+        inside = (time >= 0) & (time < SAMPLES)
+        masked[w] = jnp.where(inside, basis[...].astype(jnp.float32), 0.0).astype(jnp.bfloat16)
+
+    wide = lax.broadcasted_iota(jnp.int32, turns.shape, 1)
+    freq = jnp.where(wide % 4 < 2, lax.broadcasted_iota(jnp.int32, turns.shape, 0) + F0, 1)
+    shift = jnp.zeros(turns.shape, jnp.int32)
+    for w in range(windows):
+        shift = jnp.where(wide // 4 == w, offsets[w], shift)
+    turn = (freq * shift).astype(jnp.float32)
+    turn = turn - SAMPLES * jnp.floor(turn * (1 / SAMPLES))
+    turn = turn * (2 * math.pi / SAMPLES) - jnp.where(wide % 2 == 1, math.pi / 2, 0.0)
+    turns[...] = jnp.cos(turn)
+
     lane = lax.broadcasted_iota(jnp.int32, (16, 128), 1)
     columns[:, 48:, :] = jnp.zeros((GROUPS, 16, 128), jnp.float32)
 
@@ -98,34 +114,50 @@
         def chunk(k, _):
             load(w, k).wait()
             at = (me // 4) ^ k
-            found = jnp.dot(basis[w], held[w, k], preferred_element_type=jnp.float32)
+            found = jnp.dot(masked[w], held[w, k], preferred_element_type=jnp.float32)
             found = (found[:RANK] + found[RANK:]).astype(jnp.bfloat16)
             for i in range(4):
                 part = found[:, 256 * i : 256 * (i + 1)]
                 message[w, at * 4 + i, :, 0:256] = part[:16]
                 message[w, at * 4 + i, :, 256:512] = part[16:]
             for i in range(8):
-                coded[at * 8 + i] = found[:, 128 * i : 128 * (i + 1)]
+                coded[w, at * 8 + i] = found[:, 128 * i : 128 * (i + 1)]
             return 0
 
         lax.fori_loop(0, chunks, chunk, 0)
 
+        arrived[w, me] = message[w, me]
+
+    def choose(w):
+        wide = lax.broadcasted_iota(jnp.int32, (RANK, 128), 1)
+
         def pick(i, total):
-            tile = coded[picks[0, i]].astype(jnp.float32)
-            wide = lax.broadcasted_iota(jnp.int32, (RANK, 128), 1)
-            value = jnp.sum(jnp.where(wide == picks[1, i], tile, 0.0), axis=1, keepdims=True)
             slot = i // 12 * SLOTS + i % 12
+            source = sources[i % 12 // slots, i // 12 * slots + i % slots]
+            tile = coded[w, source // 128].astype(jnp.float32)
+            value = jnp.sum(jnp.where(wide == source % 128, tile, 0.0), axis=1, keepdims=True)
             total = jnp.where(lane == slot, value[:16], total)
             return jnp.where(lane == slot + 64, value[16:], total)
 
-        chosen = lax.fori_loop(0, count, pick, jnp.zeros((16, 128), jnp.float32)).astype(jnp.bfloat16)
-
-        def fill(c, _):
-            message[w, c, :, 512:640] = chosen
-            return 0
-
-        lax.fori_loop(0, blocks, fill, 0)
-        arrived[w, me] = message[w, me]
+        chosen = lax.fori_loop(0, ROUNDS * slots * 4, pick, jnp.zeros((16, 128), jnp.float32), unroll=8)
+        picked[me // 8, me // 4 % 2, me % 4, w] = chosen.astype(jnp.bfloat16)
+
+    def cast(step, k):
+        x, z, y = me // 8, me // 4 % 2, me % 4
+        part = (picked.at[x, z, y], picked.at[x, :, y], picked.at[:, :, y])[step]
+        return pltpu.make_async_remote_copy(
+            part, part, pick_send.at[step, k], pick_recv.at[step, k],
+            device_id=(win, me ^ (4, 8 * k, k)[step]), device_id_type=MESH,
+        )
+
+    def caught(step, k):
+        there = me ^ (4, 8 * k, k)[step]
+        x, z, y = there // 8, there // 4 % 2, there % 4
+        part = (picked.at[x, z, y], picked.at[x, :, y], picked.at[:, :, y])[step]
+        return pltpu.make_async_remote_copy(
+            part, part, pick_send.at[step, k], pick_recv.at[step, k],
+            device_id=(win, there), device_id_type=MESH,
+        )
 
     def send(w, k):
         return pltpu.make_async_remote_copy(
@@ -149,20 +181,24 @@
     project(0)
     pl.semaphore_wait(barrier, blocks - 1 + 3)
     start_sends(0)
+    project(1)
+    start_sends(1)
+    project(2)
+    start_sends(2)
+    choose(0)
 
     def later(w, _):
-        project(w)
-        start_sends(w)
+        choose(w)
         return 0
 
     lax.fori_loop(1, windows, later, 0)
+    cast(0, 1).start()
 
     table_copy.wait()
 
-    def tabulate(i, _):
-        w, g = i // GROUPS, i % GROUPS
+    def tabulate(w, g):
         own_re, own_im, sum_re, sum_im, dif_re, dif_im = [parts[t, pl.ds(pl.multiple_of(g * 8, 8), 8)] for t in range(6)]
-        turn = turns[w, pl.ds(pl.multiple_of(g * 8, 8), 8)]
+        turn = turns[pl.ds(pl.multiple_of(g * 8, 8), 8), :][:, 4 * w : 4 * w + 4]
         c, s = turn[:, 2:3], turn[:, 3:4]
         re = own_re + c * sum_re - s * dif_im
         im = own_im + c * sum_im + s * dif_re
@@ -173,7 +209,8 @@
         full[w, 1, g] = (both - high.astype(jnp.float32)).astype(jnp.bfloat16)
         return 0
 
-    lax.fori_loop(0, windows * GROUPS, tabulate, 0)
+    for w in range(windows):
+        lax.fori_loop(0, GROUPS, lambda g, _, w=w: tabulate(w, g), 0, unroll=2)
 
     def hand(w, k):
         return pltpu.make_async_remote_copy(
@@ -196,7 +233,7 @@
     def keep(w):
         return pltpu.make_async_copy(whites.at[w], white_out.at[win, w], own_sem.at[w])
 
-    def whiten(w, _):
+    def whiten(w):
         def wait_one(k, _):
             receive(w, k).wait_recv()
             return 0
@@ -204,45 +241,71 @@
         lax.fori_loop(1, blocks, wait_one, 0)
         first = arrived[w, :, :, 0:256].reshape(blocks * 16, 256)
         second = arrived[w, :, :, 256:512].reshape(blocks * 16, 256)
-        extra = arrived[w, :, :, 512:640].reshape(blocks * 16, 128)
         cut = blocks * 16
 
         def tile(m, power):
             found = jnp.zeros((128, 256), jnp.float32)
+            for half in range(2):
+                table = full[w, half, pl.ds(m * 8, 8)].reshape(128, 2 * cut)
+                found += jnp.dot(table[:, :cut], first, preferred_element_type=jnp.float32)
+                found += jnp.dot(table[:, cut:], second, preferred_element_type=jnp.float32)
+            spectra[pl.ds(pl.multiple_of(m * 128, 128), 128)] = found
+            return power + jnp.sum(found * found, axis=0, keepdims=True)
+
+        power = lax.fori_loop(0, 4, tile, jnp.zeros((1, 256), jnp.float32))
+        scale = lax.rsqrt(power * (1 / (2 * BINS)) + 1e-06)
+
+        def norm(m, _):
+            white = (spectra[pl.ds(pl.multiple_of(m * 128, 128), 128)] * scale).astype(jnp.bfloat16)
+            whites[w, pl.ds(m * 8, 8)] = white.reshape(8, 16, 256)
+            return 0
+
+        lax.fori_loop(0, 4, norm, 0)
+        hand(w, 2).start()
+        hand(w, 1).start()
+        keep(w).start()
+
+    def whiten_picked(w, _):
+        extra = picked[:, :, :, w].reshape(blocks * 16, 128)
+        cut = blocks * 16
+
+        def tile(m, power):
             low = jnp.zeros((128, 128), jnp.float32)
             top = jnp.zeros((128, 128), jnp.float32)
             for half in range(2):
                 table = full[w, half, pl.ds(m * 8, 8)].reshape(128, 2 * cut)
-                left, right = table[:, :cut], table[:, cut:]
-                found += jnp.dot(left, first, preferred_element_type=jnp.float32)
-                found += jnp.dot(right, second, preferred_element_type=jnp.float32)
-                low += jnp.dot(left, extra, preferred_element_type=jnp.float32)
-                top += jnp.dot(right, extra, preferred_element_type=jnp.float32)
-            rows_at = pl.ds(pl.multiple_of(m * 128, 128), 128)
-            spectra[rows_at, 0:256] = found
-            mine = low + pltpu.roll(top, 64, 1)
-            spectra[rows_at, 256:384] = mine
-            return power[0] + jnp.sum(found * found, axis=0, keepdims=True), power[1] + jnp.sum(mine * mine, axis=0, keepdims=True)
-
-        zero = jnp.zeros((1, 256), jnp.float32), jnp.zeros((1, 128), jnp.float32)
-        power = lax.fori_loop(0, 4, tile, zero)
-        scale, scale_picked = [lax.rsqrt(p * (1 / (2 * BINS)) + 1e-06) for p in power]
+                low += jnp.dot(table[:, :cut], extra, preferred_element_type=jnp.float32)
+                top += jnp.dot(table[:, cut:], extra, preferred_element_type=jnp.float32)
+            found = low + pltpu.roll(top, 64, 1)
+            spectra[pl.ds(pl.multiple_of(m * 128, 128), 128), 0:128] = found
+            return power + jnp.sum(found * found, axis=0, keepdims=True)
+
+        power = lax.fori_loop(0, 4, tile, jnp.zeros((1, 128), jnp.float32))
+        scale = lax.rsqrt(power * (1 / (2 * BINS)) + 1e-06)
 
         def norm(m, _):
-            rows_at = pl.ds(pl.multiple_of(m * 128, 128), 128)
-            white = (spectra[rows_at, 0:256] * scale).astype(jnp.bfloat16)
-            whites[w, pl.ds(m * 8, 8)] = white.reshape(8, 16, 256)
-            white = (spectra[rows_at, 256:384] * scale_picked).astype(jnp.bfloat16).astype(jnp.float32)
-            columns[pl.ds(m * 8, 8), pl.ds(pl.multiple_of(w * 16, 16), 16)] = white.reshape(8, 16, 128)
+            white = spectra[pl.ds(pl.multiple_of(m * 128, 128), 128), 0:128] * scale
+            columns[pl.ds(m * 8, 8), pl.ds(pl.multiple_of(w * 16, 16), 16)] = (
+                white.astype(jnp.bfloat16).astype(jnp.float32).reshape(8, 16, 128)
+            )
             return 0
 
         lax.fori_loop(0, 4, norm, 0)
-        hand(w, 2).start()
-        hand(w, 1).start()
-        keep(w).start()
-        return 0
-
-    lax.fori_loop(0, windows, whiten, 0)
+        return 0
+
+    caught(0, 1).wait_recv()
+    for k in (2, 1, 3):
+        cast(1, k).start()
+    whiten(0)
+    for k in (1, 2, 3):
+        caught(1, k).wait_recv()
+    for k in (2, 1, 3):
+        cast(2, k).start()
+    whiten(1)
+    whiten(2)
+    for k in (1, 2, 3):
+        caught(2, k).wait_recv()
+    lax.fori_loop(0, windows, whiten_picked, 0)
 
     def turn_over(at, _):
         block = columns[pl.ds(at * 2, 2)].reshape(128, 128).T
@@ -292,12 +355,15 @@
 
     lax.fori_loop(0, windows, finish, 0)
     own_rows.wait()
+    cast(0, 1).wait_send()
     for k in (1, 2, 3):
+        cast(1, k).wait_send()
+        cast(2, k).wait_send()
         deal(k).wait_send()
         dealt(k).wait_recv()
 
 
-def exchanged(record, tables, basis, turns, picks, blocks, hosts):
+def exchanged(record, tables, basis, offsets, sources, blocks, hosts):
     windows, count, channels = record.shape
     width = channels // blocks
     dma = pltpu.SemaphoreType.DMA
@@ -312,18 +378,21 @@
             anywhere,
             anywhere,
             pl.BlockSpec(memory_space=pltpu.VMEM),
-            pl.BlockSpec(memory_space=pltpu.VMEM),
+            pl.BlockSpec(memory_space=pltpu.SMEM),
             pl.BlockSpec(memory_space=pltpu.SMEM),
         ],
         out_specs=(anywhere, anywhere),
         scratch_shapes=[
             pltpu.VMEM((windows, 8, count, channels // 8), jnp.bfloat16),
             pltpu.VMEM(tables.shape, jnp.float32),
-            pltpu.VMEM((windows, blocks, 16, 640), jnp.bfloat16),
-            pltpu.VMEM((windows, blocks, 16, 640), jnp.bfloat16),
-            pltpu.VMEM((channels // 128, RANK, 128), jnp.bfloat16),
+            pltpu.VMEM((windows,) + basis.shape, jnp.bfloat16),
+            pltpu.VMEM((BINS, 128), jnp.float32),
+            pltpu.VMEM((windows, blocks, 16, 2 * width), jnp.bfloat16),
+            pltpu.VMEM((windows, blocks, 16, 2 * width), jnp.bfloat16),
+            pltpu.VMEM((windows, channels // 128, RANK, 128), jnp.bfloat16),
+            pltpu.VMEM((4, 2, 4, windows, 16, 128), jnp.bfloat16),
             pltpu.VMEM((windows, 2, GROUPS, 16, blocks * RANK), jnp.bfloat16),
-            pltpu.VMEM((2 * BINS, 384), jnp.float32),
+            pltpu.VMEM((2 * BINS, width), jnp.float32),
             pltpu.VMEM((GROUPS, 64, 128), jnp.float32),
             pltpu.VMEM((windows, GROUPS, 16, width), jnp.bfloat16),
             pltpu.VMEM((hosts, GROUPS // 2, SLOTS, 128), jnp.bfloat16),
@@ -336,9 +405,11 @@
             dma((4,)),
             dma((4,)),
             dma((windows,)),
+            dma((3, 4)),
+            dma((3, 4)),
         ],
         compiler_params=pltpu.CompilerParams(collective_id=0, has_side_effects=True, vmem_limit_bytes=48 << 20),
-    )(record, tables, basis, turns, picks)
+    )(record, tables, basis, offsets, sources)
 
 
 def correlate(white_ref, rows_ref, lag_ref, out_ref, cross):
@@ -377,7 +448,7 @@
                 cross[:, group] = found.astype(jnp.bfloat16).reshape(used, 16, -1)
             return 0
 
-        lax.fori_loop(0, GROUPS // 2, pair, 0)
+        lax.fori_loop(0, GROUPS // 2, pair, 0, unroll=4)
 
     spectrum = cross[pl.program_id(0)].reshape(2 * BINS, -1)
     found = jnp.dot(lag_ref[...], spectrum, preferred_element_type=jnp.float32)
@@ -386,7 +457,7 @@
 
 def correlations(white, rows, total, used):
     hosts, windows, _, _, width = white.shape
-    lags = split_pair(jnp.asarray(lag_matrix(1 / math.sqrt(total * BINS))))
+    lags = jnp.asarray(np.concatenate(split_pair(lag_matrix(1 / math.sqrt(total * BINS)))))
     return pl.pallas_call(
         correlate,
         grid=(used,),
@@ -399,34 +470,17 @@
         out_specs=pl.BlockSpec((1, LAGS, width), lambda s: (s, 0, 0)),
         scratch_shapes=[pltpu.VMEM((used, GROUPS, 16, width), jnp.bfloat16)],
         compiler_params=pltpu.CompilerParams(vmem_limit_bytes=32 << 20),
-    )(white, rows, jnp.concatenate(lags, axis=0))
+    )(white, rows, lags)
 
 
 def body(record, offsets, sources):
     windows, count, channels = record.shape
     blocks, hosts = lax.axis_size("chan"), lax.axis_size("win")
     width = channels // blocks
-    first = lax.axis_index("chan") * count
-
-    at = first + jnp.arange(count, dtype=jnp.int32)[None, :] - offsets[:, None]
-    inside = (at >= 0) & (at < SAMPLES)
-    basis = sample_basis(count).T.astype(np.float32)
-    high = basis.astype(jnp.bfloat16)
-    low = (basis - high.astype(np.float32)).astype(jnp.bfloat16)
-    basis = jnp.where(inside[:, None, :], jnp.asarray(np.concatenate([high, low]))[None], 0.0)
-
     per = sources.shape[1] // hosts
-    wanted = sources.reshape(ROUNDS, hosts, per).transpose(1, 0, 2).reshape(-1)
-    picks = jnp.stack([wanted // 128, wanted % 128])
-
-    freqs = jnp.arange(BINS, dtype=jnp.int32) + F0
-    turn = 2 * math.pi / SAMPLES * (freqs[None, :] * offsets[:, None] % SAMPLES).astype(jnp.float32)
-    step = jnp.broadcast_to(2 * math.pi / SAMPLES * offsets.astype(jnp.float32)[:, None], turn.shape)
-    turns = jnp.stack([jnp.cos(turn), jnp.sin(turn), jnp.cos(step), jnp.sin(step)], axis=2)
-    turns = jnp.pad(turns, ((0, 0), (0, 0), (0, 124)))
-
+    basis = jnp.asarray(np.concatenate(split_pair(sample_basis(count).T)))
     tables = jnp.asarray(spectrum_tables(count, blocks))
-    white, rows = exchanged(record, tables, basis, turns, picks, blocks, hosts)
+    white, rows = exchanged(record, tables, basis, offsets, sources, blocks, hosts)
     out = correlations(white, rows, windows * hosts, ROUNDS * per)
     return out.reshape(ROUNDS, per, LAGS, width)
 

time: 75.8 us -> 64.2 us (0.85)
  Pallas kernels: 71.2 us -> 61.9 us
  other arithmetic: 3.09 us -> 0 us
  local copies, waits for them, and re-layouts: 1.22 us -> 2.16 us
    pallas_call x1, Pallas kernels: 59.8 us -> 53.4 us  [exchanged(): pl.pallas_call(exchange, out_shape=(jax.ShapeDtypeStruct((hosts, windows,...]
    pallas_call x1, Pallas kernels: 11.5 us -> 8.5 us  [correlations(): pl.pallas_call(correlate, grid=(used,), out_shape=jax.ShapeDtypeStruct((u...]
    unnamed x2 -> x8, local copies, waits for them, and re-layouts: 0.01 us -> 2.16 us
    cos x2 -> x0, other arithmetic: 1.54 us -> none  [the longest x1 0.84 us: body(): jnp.cos(turn)]
    reshape x2 -> x0, local copies, waits for them, and re-layouts: 0.85 us -> none  [body(): wanted = sources.reshape(ROUNDS, hosts, per).transpose(1, 0, 2).reshape(-1)]
    select_n x2 -> x0, other arithmetic: 0.78 us -> none  [the longest x1 0.77 us: body(): jnp.where(inside[:, None, :], jnp.asarray(np.concatenate([high, low]))[No...]
where the time goes in v4:
time: 64.2 us; the launch traced here: 64.1 us
  Pallas kernels  61.9 us (96%)
  local copies, waits for them, and re-layouts  2.16 us (3%)
    pallas_call x1, Pallas kernels, exchanged(): pl.pallas_call(exchange, out_shape=(jax.ShapeDtypeStruct((hosts, windows,...  53.4 us
    pallas_call x1, Pallas kernels, correlations(): pl.pallas_call(correlate, grid=(used,), out_shape=jax.ShapeDtypeStruct((u...  8.5 us
    unnamed x8, local copies, waits for them, and re-layouts  2.16 us

profile of v4, /device:TPU:1, one launch (start us, length us, event | category | flops | bytes accessed | tf_op | source)
XLA Modules:
  0.0 64.1 jit_solution(1405351090322617261)
XLA Ops:
  0.0 0.0 copy-start
  0.0 0.0 copy-start.1
  0.0 0.8 %copy-done.1 = bf16[64,248]{1,0:T(8,128)(2,1)S(1)} copy-done((bf16[64,248]{1,0:T(8,128)(2,1)S(1)}, bf16[64,248]{1,0:T(8,128)(2,1)}, u32[]{:S(2)}) %copy-start.1) | copy-done | bytes 31768
  0.8 0.0 copy-start.2
  0.8 0.7 %copy-done.2 = s32[3,16]{1,0:T(4,128)S(1)} copy-done((s32[3,16]{1,0:T(4,128)S(1)}, s32[3,16]{1,0:T(4,128)}, u32[]{:S(2)}) %copy-start.2) | copy-done | bytes 216
  1.5 0.0 copy-start.3
  1.5 0.7 %copy-done.3 = s32[3]{0:T(128)S(1)} copy-done((s32[3]{0:T(128)S(1)}, s32[3]{0:T(128)}, u32[]{:S(2)}) %copy-start.3) | copy-done | bytes 36
  2.2 53.4 %shard_map.64 = (bf16[4,3,32,16,256]{4,3,2,1,0:T(8,128)(2,1)S(1)}, bf16[4,16,16,128]{3,2,1,0:T(8,128)(2,1)S(1)}) custom-call(bf16[3,248,8192]{2,1,0:T(8,128)(2,1)} %record.1, f32[6,256,1024]{2,1,0:T(8,128)} %constant.7.clone.tables, bf16[64,248]{1,0:T(8,128)(2,1)S(1)} %copy-done.1, s32[3]{0:T(128)S(1)} %copy-done.3, s32[3,16]{1,0:T(4,128)S(1)} %copy-done.2), custom_call_target="tpu_custom_call" | custom-call | tf_op jit(solution)/shard_map/pallas_call | solution.py:371
  55.6 0.0 copy-done
  55.6 8.5 %shard_map.65 = bf16[12,256,256]{2,1,0:T(8,128)(2,1)} custom-call(bf16[4,3,32,16,256]{4,3,2,1,0:T(8,128)(2,1)S(1)} %get-tuple-element.7.white_ref, bf16[4,16,16,128]{3,2,1,0:T(8,128)(2,1)S(1)} %get-tuple-element.8.rows_ref, bf16[512,512]{1,0:T(8,128)(2,1)S(1)} %copy-done), custom_call_target="tpu_custom_call" | custom-call | tf_op jit(solution)/shard_map/pallas_call | solution.py:461
Async XLA Ops:
  0.0 55.6 %copy-start = (bf16[512,512]{1,0:T(8,128)(2,1)S(1)}, bf16[512,512]{1,0:T(8,128)(2,1)}, u32[]{:S(2)}) copy-start(bf16[512,512]{1,0:T(8,128)(2,1)} %constant.8.clone.lag_ref) | copy-start | bytes 1572868
  0.0 0.8 %copy-start.1 = (bf16[64,248]{1,0:T(8,128)(2,1)S(1)}, bf16[64,248]{1,0:T(8,128)(2,1)}, u32[]{:S(2)}) copy-start(bf16[64,248]{1,0:T(8,128)(2,1)} %constant.6.clone.basis) | copy-start | bytes 95236
  0.8 0.7 %copy-start.2 = (s32[3,16]{1,0:T(4,128)S(1)}, s32[3,16]{1,0:T(4,128)}, u32[]{:S(2)}) copy-start(s32[3,16]{1,0:T(4,128)} %sources.1) | copy-start | bytes 580
  1.5 0.7 %copy-start.3 = (s32[3]{0:T(128)S(1)}, s32[3]{0:T(128)}, u32[]{:S(2)}) copy-start(s32[3]{0:T(128)} %offsets.1) | copy-start | bytes 40

commit v5 on v4

v5 whole, which is shorter than its diff:
```python
import math

import jax
import jax.numpy as jnp
import numpy as np
from jax import lax
from jax.experimental import pallas as pl
from jax.experimental.pallas import tpu as pltpu
from jax.sharding import PartitionSpec as P

SAMPLES = 7680
BINS = 256
F0 = 16
LAGS = 256
LAG_STEP = 8
ROUNDS = 3
RANK = 32
GROUPS = BINS // 8
SLOTS = 16
PIECES = 4
EARLY = 2
MESH = pl.DeviceIdType.MESH


def sample_basis(count):
    half = (F0 + BINS) / SAMPLES
    at = np.arange(count)
    matrix = np.diag(((count - 1) / 2 - at) ** 2 * math.cos(2 * math.pi * half))
    side = at[1:] * (count - at[1:]) / 2
    matrix = matrix + np.diag(side, 1) + np.diag(side, -1)
    vectors = np.linalg.eigh(matrix)[1][:, ::-1][:, :RANK]
    return vectors * np.where(vectors[0] < 0, -1.0, 1.0)


def spectrum_tables(count, blocks):
    basis = sample_basis(count)
    middle = (count - 1) / 2
    at = np.arange(count) - middle
    terms = []
    for step, weight in ((0, 0.5), (1, -0.25), (-1, -0.25)):
        freqs = np.arange(BINS) + F0 + step
        wave = np.exp(-2j * math.pi / SAMPLES * np.outer(freqs, at)) @ basis
        turn = np.exp(-2j * math.pi / SAMPLES * np.outer(freqs, count * np.arange(blocks) + middle))
        table = weight * (turn[:, :, None] * wave[:, None, :]).reshape(BINS, blocks, 2, RANK // 2)
        terms.append(table.transpose(0, 2, 1, 3).reshape(BINS, blocks * RANK))
    own, above, below = terms
    return np.stack([p for t in (own, above + below, above - below) for p in (t.real, t.imag)]).astype(np.float32)


def lag_matrix(scale):
    shifts = LAG_STEP * (np.arange(LAGS) - LAGS // 2)
    phase = shifts[:, None] * (np.arange(BINS) + F0)[None, :] % SAMPLES
    angle = 2 * math.pi / SAMPLES * phase
    both = np.stack([np.cos(angle), np.sin(angle)], axis=1).reshape(LAGS, 2, GROUPS, 8)
    return (both.transpose(0, 2, 1, 3).reshape(LAGS, 2 * BINS) * scale).astype(np.float32)


def split_pair(array):
    high = array.astype(jnp.bfloat16)
    return high, (array - high.astype(array.dtype)).astype(jnp.bfloat16)


def exchange(
    record, tables, basis_in, lags_in, offsets_in, sources_in, out,
    held, parts, basis, lags, offsets, sources, masked, turns, message, arrived, coded, picked, full, spectra, columns,
    white, rows, rows_in, spread, cross, partial, done,
    load_sem, const_sem, send_sem, recv_sem, pass_sem, take_sem, rows_send, rows_recv, pick_send, pick_recv, out_sem,
):
    windows, chunks = held.shape[:2]
    blocks = message.shape[1]
    samples = held.shape[2]
    slots = sources.shape[1] // 4
    me, win = lax.axis_index("chan"), lax.axis_index("win")

    def load(w, k):
        at = (me // 4) ^ k
        source = record.at[w, :, pl.ds(pl.multiple_of(at * 1024, 1024), 1024)]
        return pltpu.make_async_copy(source, held.at[w, k], load_sem.at[w, k])

    def start_load(i, _):
        load(i // chunks, i % chunks).start()
        return 0

    lax.fori_loop(0, chunks, start_load, 0)
    pairs = ((offsets_in, offsets), (sources_in, sources), (basis_in, basis), (tables, parts), (lags_in, lags))
    consts = [pltpu.make_async_copy(a, b, const_sem.at[i]) for i, (a, b) in enumerate(pairs)]
    for copy in consts[:3]:
        copy.start()
    lax.fori_loop(chunks, windows * chunks, start_load, 0)
    for copy in consts[3:]:
        copy.start()

    barrier = pltpu.get_barrier_semaphore()

    def greet(k, _):
        pl.semaphore_signal(barrier, inc=1, device_id=(win, me ^ k), device_id_type=MESH)
        return 0

    lax.fori_loop(1, blocks, greet, 0)
    for k in (1, 2, 3):
        pl.semaphore_signal(barrier, inc=1, device_id=(win ^ k, me), device_id_type=MESH)

    for copy in consts[:3]:
        copy.wait()

    for w in range(windows):
        time = lax.broadcasted_iota(jnp.int32, basis.shape, 1) + (me * samples - offsets[w])
        inside = (time >= 0) & (time < SAMPLES)
        masked[w] = jnp.where(inside, basis[...].astype(jnp.float32), 0.0).astype(jnp.bfloat16)

    wide = lax.broadcasted_iota(jnp.int32, turns.shape, 1)
    freq = jnp.where(wide % 4 < 2, lax.broadcasted_iota(jnp.int32, turns.shape, 0) + F0, 1)
    shift = jnp.zeros(turns.shape, jnp.int32)
    for w in range(windows):
        shift = jnp.where(wide // 4 == w, offsets[w], shift)
    turn = (freq * shift).astype(jnp.float32)
    turn = turn - SAMPLES * jnp.floor(turn * (1 / SAMPLES))
    turn = turn * (2 * math.pi / SAMPLES) - jnp.where(wide % 2 == 1, math.pi / 2, 0.0)
    turns[...] = jnp.cos(turn)

    lane = lax.broadcasted_iota(jnp.int32, (16, 128), 1)
    columns[:, 48:, :] = jnp.zeros((GROUPS, 16, 128), jnp.float32)

    def project(w):
        def chunk(k, _):
            load(w, k).wait()
            at = (me // 4) ^ k
            found = jnp.dot(masked[w], held[w, k], preferred_element_type=jnp.float32)
            found = (found[:RANK] + found[RANK:]).astype(jnp.bfloat16)
            for i in range(4):
                part = found[:, 256 * i : 256 * (i + 1)]
                message[w, at * 4 + i, :, 0:256] = part[:16]
                message[w, at * 4 + i, :, 256:512] = part[16:]
            for i in range(8):
                coded[w, at * 8 + i] = found[:, 128 * i : 128 * (i + 1)]
            return 0

        lax.fori_loop(0, chunks, chunk, 0)

        arrived[w, me] = message[w, me]

    def choose(w, _):
        wide = lax.broadcasted_iota(jnp.int32, (RANK, 128), 1)

        def pick(i, total):
            slot = i // 12 * SLOTS + i % 12
            source = sources[i % 12 // slots, i // 12 * slots + i % slots]
            tile = coded[w, source // 128].astype(jnp.float32)
            value = jnp.sum(jnp.where(wide == source % 128, tile, 0.0), axis=1, keepdims=True)
            total = jnp.where(lane == slot, value[:16], total)
            return jnp.where(lane == slot + 64, value[16:], total)

        chosen = lax.fori_loop(0, ROUNDS * slots * 4, pick, jnp.zeros((16, 128), jnp.float32), unroll=8)
        picked[me // 8, me // 4 % 2, me % 4, w] = chosen.astype(jnp.bfloat16)
        return 0

    def cast(step, k):
        x, z, y = me // 8, me // 4 % 2, me % 4
        part = (picked.at[x, z, y], picked.at[x, :, y], picked.at[:, :, y])[step]
        return pltpu.make_async_remote_copy(
            part, part, pick_send.at[step, k], pick_recv.at[step, k],
            device_id=(win, me ^ (4, 8 * k, k)[step]), device_id_type=MESH,
        )

    def caught(step, k):
        there = me ^ (4, 8 * k, k)[step]
        x, z, y = there // 8, there // 4 % 2, there % 4
        part = (picked.at[x, z, y], picked.at[x, :, y], picked.at[:, :, y])[step]
        return pltpu.make_async_remote_copy(
            part, part, pick_send.at[step, k], pick_recv.at[step, k],
            device_id=(win, there), device_id_type=MESH,
        )

    def send(w, k):
        return pltpu.make_async_remote_copy(
            message.at[w, me ^ k], arrived.at[w, me], send_sem.at[w, k], recv_sem.at[w, me],
            device_id=(win, me ^ k), device_id_type=MESH,
        )

    def receive(w, k):
        return pltpu.make_async_remote_copy(
            message.at[w, me ^ k], arrived.at[w, me ^ k], send_sem.at[w, k], recv_sem.at[w, me ^ k],
            device_id=(win, me ^ k), device_id_type=MESH,
        )

    def start_sends(w):
        def one(k, _):
            send(w, k).start()
            return 0

        lax.fori_loop(1, blocks, one, 0, unroll=8)

    project(0)
    pl.semaphore_wait(barrier, blocks - 1 + 3)
    start_sends(0)
    project(1)
    start_sends(1)
    project(2)
    lax.fori_loop(0, windows, choose, 0)
    cast(0, 1).start()
    start_sends(2)

    consts[3].wait()

    def tabulate(w, g):
        own_re, own_im, sum_re, sum_im, dif_re, dif_im = [parts[t, pl.ds(pl.multiple_of(g * 8, 8), 8)] for t in range(6)]
        turn = turns[pl.ds(pl.multiple_of(g * 8, 8), 8), :][:, 4 * w : 4 * w + 4]
        c, s = turn[:, 2:3], turn[:, 3:4]
        re = own_re + c * sum_re - s * dif_im
        im = own_im + c * sum_im + s * dif_re
        c, s = turn[:, 0:1], turn[:, 1:2]
        both = jnp.concatenate([c * re - s * im, c * im + s * re], axis=0)
        high = both.astype(jnp.bfloat16)
        full[w, 0, g] = high
        full[w, 1, g] = (both - high.astype(jnp.float32)).astype(jnp.bfloat16)
        return 0

    for w in range(windows):
        lax.fori_loop(0, GROUPS, lambda g, _, w=w: tabulate(w, g), 0, unroll=4)

    piece = GROUPS // PIECES

    def hand(w, k, p):
        part = pl.ds(p * piece, piece)
        return pltpu.make_async_remote_copy(
            white.at[0, w, part], white.at[k, w, part], pass_sem.at[k - 1, w, p], take_sem.at[k - 1, w, p],
            device_id=(win ^ k, me), device_id_type=MESH,
        )

    def relay(w, p):
        part = pl.ds(p * piece, piece)
        return pltpu.make_async_remote_copy(
            white.at[2, w, part], white.at[3, w, part], pass_sem.at[2, w, p], take_sem.at[2, w, p],
            device_id=(win ^ 1, me), device_id_type=MESH,
        )

    def whiten(w):
        def wait_one(k, _):
            receive(w, k).wait_recv()
            return 0

        lax.fori_loop(1, blocks, wait_one, 0, unroll=8)
        first = arrived[w, :, :, 0:256].reshape(blocks * 16, 256)
        second = arrived[w, :, :, 256:512].reshape(blocks * 16, 256)
        cut = blocks * 16

        def tile(m, power):
            found = jnp.zeros((128, 256), jnp.float32)
            for half in range(2):
                table = full[w, half, pl.ds(m * 8, 8)].reshape(128, 2 * cut)
                found += jnp.dot(table[:, :cut], first, preferred_element_type=jnp.float32)
                found += jnp.dot(table[:, cut:], second, preferred_element_type=jnp.float32)
            spectra[pl.ds(pl.multiple_of(m * 128, 128), 128)] = found
            return power + jnp.sum(found * found, axis=0, keepdims=True)

        power = lax.fori_loop(0, 4, tile, jnp.zeros((1, 256), jnp.float32))
        scale = lax.rsqrt(power * (1 / (2 * BINS)) + 1e-06)

        def norm(m, _):
            found = (spectra[pl.ds(pl.multiple_of(m * 128, 128), 128)] * scale).astype(jnp.bfloat16)
            white[0, w, pl.ds(m * 8, 8)] = found.reshape(8, 16, 256)
            return 0

        lax.fori_loop(0, 4, norm, 0, unroll=2)
        for p in range(PIECES if w < windows - 1 else EARLY):
            hand(w, 2, p).start()
            hand(w, 1, p).start()

    def whiten_picked(w, _):
        extra = picked[:, :, :, w].reshape(blocks * 16, 128)
        cut = blocks * 16

        def tile(m, power):
            low = jnp.zeros((128, 128), jnp.float32)
            top = jnp.zeros((128, 128), jnp.float32)
            for half in range(1):
                table = full[w, half, pl.ds(m * 8, 8)].reshape(128, 2 * cut)
                low += jnp.dot(table[:, :cut], extra, preferred_element_type=jnp.float32)
                top += jnp.dot(table[:, cut:], extra, preferred_element_type=jnp.float32)
            found = low + pltpu.roll(top, 64, 1)
            spectra[pl.ds(pl.multiple_of(m * 128, 128), 128), 0:128] = found
            return power + jnp.sum(found * found, axis=0, keepdims=True)

        power = lax.fori_loop(0, 4, tile, jnp.zeros((1, 128), jnp.float32))
        scale = lax.rsqrt(power * (1 / (2 * BINS)) + 1e-06)

        def norm(m, _):
            found = spectra[pl.ds(pl.multiple_of(m * 128, 128), 128), 0:128] * scale
            columns[pl.ds(m * 8, 8), pl.ds(pl.multiple_of(w * 16, 16), 16)] = (
                found.astype(jnp.bfloat16).astype(jnp.float32).reshape(8, 16, 128)
            )
            return 0

        lax.fori_loop(0, 4, norm, 0, unroll=2)
        return 0

    caught(0, 1).wait_recv()
    for k in (2, 1, 3):
        cast(1, k).start()
    whiten(0)
    for k in (1, 2, 3):
        caught(1, k).wait_recv()
    for k in (2, 1, 3):
        cast(2, k).start()
    whiten(1)
    whiten(2)
    for k in (1, 2, 3):
        caught(2, k).wait_recv()
    lax.fori_loop(0, windows, whiten_picked, 0)

    def turn_over(at, _):
        block = columns[pl.ds(at * 2, 2)].reshape(128, 128).T
        rows[:, at] = block[:64].reshape(4, SLOTS, 128).astype(jnp.bfloat16)
        return 0

    lax.fori_loop(0, GROUPS // 2, turn_over, 0, unroll=4)

    def deal(k):
        return pltpu.make_async_remote_copy(
            rows.at[win ^ k], rows_in.at[k], rows_send.at[k], rows_recv.at[k],
            device_id=(win ^ k, me), device_id_type=MESH,
        )

    for k in (2, 3, 1):
        deal(k).start()
    for p in range(EARLY, PIECES):
        hand(windows - 1, 2, p).start()
        hand(windows - 1, 1, p).start()
    rows_in[0] = rows[win]

    def forward(i, _):
        hand(i // PIECES, 2, i % PIECES).wait_recv()
        relay(i // PIECES, i % PIECES).start()
        return 0

    lax.fori_loop(0, (windows - 1) * PIECES, forward, 0)
    lane = lax.broadcasted_iota(jnp.int32, (SLOTS, 128), 1)
    left = lane < 64
    real = lane % 16 < 8
    own = lax.broadcasted_iota(jnp.int32, (8, 128), 1) % 8 == lax.broadcasted_iota(jnp.int32, (8, 128), 0)
    own = jnp.where(own, 1.0, 0.0).astype(jnp.float32)
    used = done.shape[0]

    def build(at, half):
        tiles = [rows_in[2 * half + j, at].astype(jnp.float32) for j in range(2)]
        for odd in range(2):
            if odd:
                both = jnp.where(left, pltpu.roll(tiles[0], 64, 1), tiles[1])
            else:
                both = jnp.where(left, tiles[0], pltpu.roll(tiles[1], 64, 1))
            turned = jnp.where(real, pltpu.roll(both, 120, 1), -pltpu.roll(both, 8, 1))
            table = jnp.stack([both[:used, None, :] * own[None], turned[:used, None, :] * own[None]], axis=1)
            spread[at * 2 + odd, :, 128 * half : 128 * (half + 1)] = table.reshape(used * 16, 128).astype(jnp.bfloat16)

    def build_half(half):
        def one(at, _):
            build(at, half)
            return 0

        lax.fori_loop(0, GROUPS // 2, one, 0, unroll=4)

    def arrive(i, _):
        hand(i // PIECES, 1, i % PIECES).wait_recv()
        relay(i // PIECES, i % PIECES).wait_recv()
        return 0

    blank = jnp.zeros((16, white.shape[4]), jnp.bfloat16)

    def multiply(g, _):
        pieces = []
        for j in range(4):
            pieces += [white[j, w, g] for w in range(windows)] + [blank]
        found = jnp.dot(spread[g], jnp.concatenate(pieces, axis=0), preferred_element_type=jnp.float32)
        cross[:, g] = found.astype(jnp.bfloat16).reshape(used, 16, -1)
        return 0

    def lagged(s, half):
        part = cross[s, GROUPS // 2 * half : GROUPS // 2 * (half + 1)].reshape(BINS, -1)
        return jnp.dot(lags[:, BINS * half : BINS * (half + 1)], part, preferred_element_type=jnp.float32)

    def leave(s):
        return pltpu.make_async_copy(done.at[s], out.at[s], out_sem.at[s])

    def first_half(s, _):
        partial[s] = lagged(s, 0)
        return 0

    def second_half(s, _):
        done[s] = (partial[s] + lagged(s, 1)).astype(jnp.bfloat16)
        leave(s).start()
        return 0

    last = (windows - 1) * PIECES
    deal(1).wait_recv()
    build_half(0)
    consts[4].wait()
    lax.fori_loop(0, last, arrive, 0)
    forward(last, 0)
    for k in (2, 3):
        deal(k).wait_recv()
    build_half(1)
    for p in range(PIECES):
        if p + 1 < PIECES:
            forward(last + p + 1, 0)
        arrive(last + p, 0)
        lax.fori_loop(p * piece, (p + 1) * piece, multiply, 0, unroll=4)
        if p == PIECES // 2 - 1:
            lax.fori_loop(0, used, first_half, 0, unroll=2)
    lax.fori_loop(0, used, second_half, 0, unroll=2)

    def finish(i, _):
        w, p = i // PIECES, i % PIECES
        hand(w, 1, p).wait_send()
        hand(w, 2, p).wait_send()
        relay(w, p).wait_send()
        return 0

    def sent(w, _):
        def one(k, _):
            send(w, k).wait_send()
            return 0

        lax.fori_loop(1, blocks, one, 0, unroll=8)
        return 0

    lax.fori_loop(0, windows * PIECES, finish, 0)
    lax.fori_loop(0, windows, sent, 0)
    cast(0, 1).wait_send()
    for k in (1, 2, 3):
        cast(1, k).wait_send()
        cast(2, k).wait_send()
        deal(k).wait_send()

    def left_all(s, _):
        leave(s).wait()
        return 0

    lax.fori_loop(0, used, left_all, 0)


def body(record, offsets, sources):
    windows, count, channels = record.shape
    blocks, hosts = lax.axis_size("chan"), lax.axis_size("win")
    width = channels // blocks
    per = sources.shape[1] // hosts
    used = ROUNDS * per
    basis = jnp.asarray(np.concatenate(split_pair(sample_basis(count).T)))
    tables = jnp.asarray(spectrum_tables(count, blocks))
    scale = 1 / math.sqrt(windows * hosts * BINS)
    lags = jnp.asarray(lag_matrix(scale).astype(jnp.bfloat16))
    dma = pltpu.SemaphoreType.DMA
    anywhere = pl.BlockSpec(memory_space=pl.ANY)
    out = pl.pallas_call(
        exchange,
        out_shape=jax.ShapeDtypeStruct((used, LAGS, width), jnp.bfloat16),
        in_specs=[anywhere] * 6,
        out_specs=anywhere,
        scratch_shapes=[
            pltpu.VMEM((windows, 8, count, channels // 8), jnp.bfloat16),
            pltpu.VMEM(tables.shape, jnp.float32),
            pltpu.VMEM(basis.shape, jnp.bfloat16),
            pltpu.VMEM(lags.shape, jnp.bfloat16),
            pltpu.SMEM(offsets.shape, jnp.int32),
            pltpu.SMEM(sources.shape, jnp.int32),
            pltpu.VMEM((windows,) + basis.shape, jnp.bfloat16),
            pltpu.VMEM((BINS, 128), jnp.float32),
            pltpu.VMEM((windows, blocks, 16, 2 * width), jnp.bfloat16),
            pltpu.VMEM((windows, blocks, 16, 2 * width), jnp.bfloat16),
            pltpu.VMEM((windows, channels // 128, RANK, 128), jnp.bfloat16),
            pltpu.VMEM((4, 2, 4, windows, 16, 128), jnp.bfloat16),
            pltpu.VMEM((windows, 2, GROUPS, 16, blocks * RANK), jnp.bfloat16),
            pltpu.VMEM((2 * BINS, width), jnp.float32),
            pltpu.VMEM((GROUPS, 64, 128), jnp.float32),
            pltpu.VMEM((hosts, windows, GROUPS, 16, width), jnp.bfloat16),
            pltpu.VMEM((hosts, GROUPS // 2, SLOTS, 128), jnp.bfloat16),
            pltpu.VMEM((hosts, GROUPS // 2, SLOTS, 128), jnp.bfloat16),
            pltpu.VMEM((GROUPS, used * 16, 256), jnp.bfloat16),
            pltpu.VMEM((used, GROUPS, 16, width), jnp.bfloat16),
            pltpu.VMEM((used, LAGS, width), jnp.float32),
            pltpu.VMEM((used, LAGS, width), jnp.bfloat16),
            dma((windows, 8)),
            dma((5,)),
            dma((windows, blocks)),
            dma((windows, blocks)),
            dma((3, windows, PIECES)),
            dma((3, windows, PIECES)),
            dma((4,)),
            dma((4,)),
            dma((3, 4)),
            dma((3, 4)),
            dma((used,)),
        ],
        compiler_params=pltpu.CompilerParams(collective_id=0, has_side_effects=True, vmem_limit_bytes=56 << 20),
    )(record, tables, basis, lags, offsets, sources)
    return out.reshape(ROUNDS, per, LAGS, width)


def solution(mesh):
    return jax.shard_map(
        body,
        mesh=mesh,
        in_specs=(P("win", "chan", None), P("win"), P()),
        out_specs=P(None, "win", None, "chan"),
        check_vma=False,
    )
```

time: 64.2 us -> 61.1 us (0.952)
  Pallas kernels: 61.9 us -> 58.3 us
    pallas_call x2 -> x1, Pallas kernels: 61.9 us -> 58.3 us  [body(): pl.pallas_call(exchange, out_shape=jax.ShapeDtypeStruct((used, LAGS, widt...]
    unnamed x8 -> x1, local copies, waits for them, and re-layouts: 2.16 us -> 2.65 us
where the time goes in v5:
time: 61.1 us; the launch traced here: 60.9 us
  Pallas kernels  58.3 us (95%)
  local copies, waits for them, and re-layouts  2.65 us (4%)
    pallas_call x1, Pallas kernels, body(): pl.pallas_call(exchange, out_shape=jax.ShapeDtypeStruct((used, LAGS, widt...  58.3 us
    unnamed x1, local copies, waits for them, and re-layouts  2.65 us

profile of v5, /device:TPU:1, one launch (start us, length us, event | category | flops | bytes accessed | tf_op | source)
XLA Modules:
  0.0 60.9 jit_solution(10313681320118467456)
XLA Ops:
  0.0 58.3 %shard_map.64 = bf16[12,256,256]{2,1,0:T(8,128)(2,1)} custom-call(bf16[3,248,8192]{2,1,0:T(8,128)(2,1)} %record.1, f32[6,256,1024]{2,1,0:T(8,128)} %constant.7.clone.tables, bf16[64,248]{1,0:T(8,128)(2,1)} %constant.6.clone.basis_in, bf16[256,512]{1,0:T(8,128)(2,1)} %constant.8.clone.lags_in, s32[3]{0:T(128)} %offsets_in.1, s32[3,16]{1,0:T(4,128)} %sources_in.1), custom_call_target="tpu_custom_call" | custom-call | tf_op jit(solution)/shard_map/pallas_call | solution.py:453
  58.3 2.7 %copy.8 = bf16[3,4,256,256]{3,2,1,0:T(8,128)(2,1)} copy(bf16[3,4,256,256]{3,2,1,0:T(8,128)(2,1)} %bitcast.1) | data formatting | bytes 3145728

commit v6 on v5

--- a/solution.py
+++ b/solution.py
@@ -18,7 +18,7 @@
 GROUPS = BINS // 8
 SLOTS = 16
 PIECES = 4
-EARLY = 2
+EARLY = 1
 MESH = pl.DeviceIdType.MESH
 
 
@@ -196,9 +196,9 @@
     project(1)
     start_sends(1)
     project(2)
+    start_sends(2)
     lax.fori_loop(0, windows, choose, 0)
     cast(0, 1).start()
-    start_sends(2)
 
     consts[3].wait()
 
@@ -396,6 +396,28 @@
     consts[4].wait()
     lax.fori_loop(0, last, arrive, 0)
     forward(last, 0)
+
+    def finish(i, _):
+        w, p = i // PIECES, i % PIECES
+        hand(w, 1, p).wait_send()
+        hand(w, 2, p).wait_send()
+        relay(w, p).wait_send()
+        return 0
+
+    def sent(w, _):
+        def one(k, _):
+            send(w, k).wait_send()
+            return 0
+
+        lax.fori_loop(1, blocks, one, 0, unroll=8)
+        return 0
+
+    lax.fori_loop(0, windows, sent, 0)
+    lax.fori_loop(0, last, finish, 0)
+    cast(0, 1).wait_send()
+    for k in (1, 2, 3):
+        cast(1, k).wait_send()
+        cast(2, k).wait_send()
     for k in (2, 3):
         deal(k).wait_recv()
     build_half(1)
@@ -408,34 +430,27 @@
             lax.fori_loop(0, used, first_half, 0, unroll=2)
     lax.fori_loop(0, used, second_half, 0, unroll=2)
 
-    def finish(i, _):
-        w, p = i // PIECES, i % PIECES
-        hand(w, 1, p).wait_send()
-        hand(w, 2, p).wait_send()
-        relay(w, p).wait_send()
-        return 0
-
-    def sent(w, _):
-        def one(k, _):
-            send(w, k).wait_send()
-            return 0
-
-        lax.fori_loop(1, blocks, one, 0, unroll=8)
-        return 0
-
-    lax.fori_loop(0, windows * PIECES, finish, 0)
-    lax.fori_loop(0, windows, sent, 0)
-    cast(0, 1).wait_send()
     for k in (1, 2, 3):
-        cast(1, k).wait_send()
-        cast(2, k).wait_send()
         deal(k).wait_send()
+    lax.fori_loop(last, windows * PIECES, finish, 0)
 
     def left_all(s, _):
         leave(s).wait()
         return 0
 
     lax.fori_loop(0, used, left_all, 0)
+
+
+def duplicate(source, target, held, load_sem, store_sem):
+    loads = [pltpu.make_async_copy(source.at[i], held.at[i], load_sem.at[i]) for i in range(source.shape[0])]
+    stores = [pltpu.make_async_copy(held.at[i], target.at[i], store_sem.at[i]) for i in range(source.shape[0])]
+    for load in loads:
+        load.start()
+    for load, store in zip(loads, stores):
+        load.wait()
+        store.start()
+    for store in stores:
+        store.wait()
 
 
 def body(record, offsets, sources):
@@ -492,6 +507,13 @@
         ],
         compiler_params=pltpu.CompilerParams(collective_id=0, has_side_effects=True, vmem_limit_bytes=56 << 20),
     )(record, tables, basis, lags, offsets, sources)
+    out = pl.pallas_call(
+        duplicate,
+        out_shape=jax.ShapeDtypeStruct(out.shape, out.dtype),
+        in_specs=[anywhere],
+        out_specs=anywhere,
+        scratch_shapes=[pltpu.VMEM(out.shape, out.dtype), dma((used,)), dma((used,))],
+    )(out)
     return out.reshape(ROUNDS, per, LAGS, width)
 
 

time: 61.1 us -> 60 us (0.982)
  local copies, waits for them, and re-layouts: 2.65 us -> 0 us
  Pallas kernels: 58.3 us -> 59.9 us
    unnamed x1 -> x0, local copies, waits for them, and re-layouts: 2.65 us -> none
    pallas_call x0 -> x1, Pallas kernels: none -> 2.33 us  [body(): pl.pallas_call(duplicate, out_shape=jax.ShapeDtypeStruct(out.shape, out.d...]
    pallas_call x1, Pallas kernels: 58.3 us -> 57.6 us  [body(): pl.pallas_call(exchange, out_shape=jax.ShapeDtypeStruct((used, LAGS, widt...]
where the time goes in v6:
time: 60 us; the launch traced here: 59.9 us
  Pallas kernels  59.9 us (100%)
    pallas_call x1, Pallas kernels, body(): pl.pallas_call(exchange, out_shape=jax.ShapeDtypeStruct((used, LAGS, widt...  57.6 us
    pallas_call x1, Pallas kernels, body(): pl.pallas_call(duplicate, out_shape=jax.ShapeDtypeStruct(out.shape, out.d...  2.33 us

profile of v6, /device:TPU:1, one launch (start us, length us, event | category | flops | bytes accessed | tf_op | source)
XLA Modules:
  0.0 59.9 jit_solution(2937458952012654601)
XLA Ops:
  0.0 57.6 %shard_map.64.source = bf16[12,256,256]{2,1,0:T(8,128)(2,1)} custom-call(bf16[3,248,8192]{2,1,0:T(8,128)(2,1)} %record.1, f32[6,256,1024]{2,1,0:T(8,128)} %constant.7.clone.tables, bf16[64,248]{1,0:T(8,128)(2,1)} %constant.6.clone.basis_in, bf16[256,512]{1,0:T(8,128)(2,1)} %constant.8.clone.lags_in, s32[3]{0:T(128)} %offsets_in.1, s32[3,16]{1,0:T(4,128)} %sources_in.1), custom_call_target="tpu_custom_call" | custom-call | tf_op jit(solution)/shard_map/pallas_call | solution.py:468
  57.6 2.3 %shard_map.65 = bf16[12,256,256]{2,1,0:T(8,128)(2,1)} custom-call(bf16[12,256,256]{2,1,0:T(8,128)(2,1)} %shard_map.64.source), custom_call_target="tpu_custom_call" | custom-call | tf_op jit(solution)/shard_map/pallas_call | solution.py:510

commit v7 on v6

--- a/solution.py
+++ b/solution.py
@@ -264,6 +264,7 @@
         lax.fori_loop(0, 4, norm, 0, unroll=2)
         for p in range(PIECES if w < windows - 1 else EARLY):
             hand(w, 2, p).start()
+        for p in range(PIECES if w < windows - 1 else EARLY):
             hand(w, 1, p).start()
 
     def whiten_picked(w, _):

time: 60 us -> 60 us (level)
  no operation moved by 1% of the time
where the time goes in v7:
time: 60 us; the launch traced here: 59.9 us
  Pallas kernels  59.9 us (100%)
    pallas_call x1, Pallas kernels, body(): pl.pallas_call(exchange, out_shape=jax.ShapeDtypeStruct((used, LAGS, widt...  57.6 us
    pallas_call x1, Pallas kernels, body(): pl.pallas_call(duplicate, out_shape=jax.ShapeDtypeStruct(out.shape, out.d...  2.33 us

profile of v7, /device:TPU:1, one launch (start us, length us, event | category | flops | bytes accessed | tf_op | source)
XLA Modules:
  0.0 59.9 jit_solution(1719125618358074046)
XLA Ops:
  0.0 57.6 %shard_map.64.source = bf16[12,256,256]{2,1,0:T(8,128)(2,1)} custom-call(bf16[3,248,8192]{2,1,0:T(8,128)(2,1)} %record.1, f32[6,256,1024]{2,1,0:T(8,128)} %constant.7.clone.tables, bf16[64,248]{1,0:T(8,128)(2,1)} %constant.6.clone.basis_in, bf16[256,512]{1,0:T(8,128)(2,1)} %constant.8.clone.lags_in, s32[3]{0:T(128)} %offsets_in.1, s32[3,16]{1,0:T(4,128)} %sources_in.1), custom_call_target="tpu_custom_call" | custom-call | tf_op jit(solution)/shard_map/pallas_call | solution.py:469
  57.6 2.3 %shard_map.65 = bf16[12,256,256]{2,1,0:T(8,128)(2,1)} custom-call(bf16[12,256,256]{2,1,0:T(8,128)(2,1)} %shard_map.64.source), custom_call_target="tpu_custom_call" | custom-call | tf_op jit(solution)/shard_map/pallas_call | solution.py:511

commit v8 on v7

--- a/solution.py
+++ b/solution.py
@@ -215,8 +215,6 @@
         full[w, 1, g] = (both - high.astype(jnp.float32)).astype(jnp.bfloat16)
         return 0
 
-    for w in range(windows):
-        lax.fori_loop(0, GROUPS, lambda g, _, w=w: tabulate(w, g), 0, unroll=4)
 
     piece = GROUPS // PIECES
 
@@ -295,15 +293,18 @@
         lax.fori_loop(0, 4, norm, 0, unroll=2)
         return 0
 
+    lax.fori_loop(0, GROUPS, lambda g, _: tabulate(0, g), 0, unroll=4)
     caught(0, 1).wait_recv()
     for k in (2, 1, 3):
         cast(1, k).start()
     whiten(0)
+    lax.fori_loop(0, GROUPS, lambda g, _: tabulate(1, g), 0, unroll=4)
     for k in (1, 2, 3):
         caught(1, k).wait_recv()
     for k in (2, 1, 3):
         cast(2, k).start()
     whiten(1)
+    lax.fori_loop(0, GROUPS, lambda g, _: tabulate(2, g), 0, unroll=4)
     whiten(2)
     for k in (1, 2, 3):
         caught(2, k).wait_recv()

time: 60 us -> 60 us (level)
  no operation moved by 1% of the time
where the time goes in v8:
time: 60 us; the launch traced here: 59.9 us
  Pallas kernels  59.9 us (100%)
    pallas_call x1, Pallas kernels, body(): pl.pallas_call(exchange, out_shape=jax.ShapeDtypeStruct((used, LAGS, widt...  57.6 us
    pallas_call x1, Pallas kernels, body(): pl.pallas_call(duplicate, out_shape=jax.ShapeDtypeStruct(out.shape, out.d...  2.33 us

profile of v8, /device:TPU:1, one launch (start us, length us, event | category | flops | bytes accessed | tf_op | source)
XLA Modules:
  0.0 59.9 jit_solution(378072553076092213)
XLA Ops:
  0.0 57.6 %shard_map.64.source = bf16[12,256,256]{2,1,0:T(8,128)(2,1)} custom-call(bf16[3,248,8192]{2,1,0:T(8,128)(2,1)} %record.1, f32[6,256,1024]{2,1,0:T(8,128)} %constant.7.clone.tables, bf16[64,248]{1,0:T(8,128)(2,1)} %constant.6.clone.basis_in, bf16[256,512]{1,0:T(8,128)(2,1)} %constant.8.clone.lags_in, s32[3]{0:T(128)} %offsets_in.1, s32[3,16]{1,0:T(4,128)} %sources_in.1), custom_call_target="tpu_custom_call" | custom-call | tf_op jit(solution)/shard_map/pallas_call | solution.py:470
  57.6 2.3 %shard_map.65 = bf16[12,256,256]{2,1,0:T(8,128)(2,1)} custom-call(bf16[12,256,256]{2,1,0:T(8,128)(2,1)} %shard_map.64.source), custom_call_target="tpu_custom_call" | custom-call | tf_op jit(solution)/shard_map/pallas_call | solution.py:512
